TPU v7x, 32 devices: a whole 2x2x4 slice. The times are simulated.
32 devices in a mesh: dp: 8 (over z, y), fsdp: 4 (over x, core).
Axes of the slice: x: 2, y: 2, z: 4, core: 2. Of those that a mesh axis runs over, the one named last changes fastest.
Arguments:
- frames: bfloat16 [2, 32, 256, 1024], P(None, ('dp', 'fsdp')), may hold values from -6 to 6
- skip: bfloat16 [2, 32, 256, 1024], P(None, ('dp', 'fsdp')), may hold values from -6 to 6
- cotangent: bfloat16 [2, 32, 256, 1024], P(None, ('dp', 'fsdp')), may hold values from -6 to 6
- segment_ids: int32 [2, 32, 256], P(None, ('dp', 'fsdp')), may hold values from 0 to 3, never falling along the last dimension, each value on 1 to 128 neighbouring positions
- row_lengths: int32 [2, 32], P(None, ('dp', 'fsdp')), may hold values from 128 to 256
- w_skip: bfloat16 [2048, 1024], P(('dp', 'fsdp')), may hold values from -0.125 to 0.125
- b_skip: bfloat16 [1024], P(('dp', 'fsdp')), may hold values from -1.1953125 to 1.1953125
- gain_one: bfloat16 [1024], P(('dp', 'fsdp')), may hold values from 0.25 to 1.75
- w_qkv: bfloat16 [1024, 3072], P(('dp', 'fsdp')), may hold values from -0.1875 to 0.1875
- w_out: bfloat16 [1024, 1024], P(('dp', 'fsdp')), may hold values from -0.5 to 0.5
- gain_two: bfloat16 [1024], P(('dp', 'fsdp')), may hold values from 0.25 to 1.75
- w_up: bfloat16 [1024, 4096], P(('dp', 'fsdp')), may hold values from -0.1875 to 0.1875
- b_up: bfloat16 [4096], P(('dp', 'fsdp')), may hold values from -1.1953125 to 1.1953125
- w_down: bfloat16 [4096, 1024], P(('dp', 'fsdp')), may hold values from -0.09375 to 0.09375
- b_down: bfloat16 [1024], P(('dp', 'fsdp')), may hold values from -1.1953125 to 1.1953125
Outputs:
- output: bfloat16 [2, 32, 256, 1024], P(None, ('dp', 'fsdp'))
- frames_grad: float32 [2, 32, 256, 1024], P(None, ('dp', 'fsdp'))
- skip_grad: float32 [2, 32, 256, 1024], P(None, ('dp', 'fsdp'))
- w_skip_grad: float32 [2048, 1024], P(('dp', 'fsdp'))
- b_skip_grad: float32 [1024], P(('dp', 'fsdp'))
- gain_one_grad: float32 [1024], P(('dp', 'fsdp'))
- w_qkv_grad: float32 [1024, 3072], P(('dp', 'fsdp'))
- w_out_grad: float32 [1024, 1024], P(('dp', 'fsdp'))
- gain_two_grad: float32 [1024], P(('dp', 'fsdp'))
- w_up_grad: float32 [1024, 4096], P(('dp', 'fsdp'))
- b_up_grad: float32 [4096], P(('dp', 'fsdp'))
- w_down_grad: float32 [4096, 1024], P(('dp', 'fsdp'))
- b_down_grad: float32 [1024], P(('dp', 'fsdp'))
All inputs are finite; a program needn't handle non-finite values.
Results may differ from a plain program's by a relative error of at most 0.012.
Values may be sent and summed in bfloat16 or wider, within the bound.
No kernel may reach another device: no remote copies, remote signals or barrier semaphores. Data moves between devices by JAX's collectives and lax.ppermute only.
A program may use at most 256 MiB of HBM per device.

v0:
```python
import math

import jax
import jax.numpy as jnp
from jax import lax
from jax.sharding import PartitionSpec as P

HEADS = 16
HEAD = 64


EPSILON = 1e-06


def gelu_tanh(values):
    return (
        0.5
        * values
        * (1.0 + jnp.tanh(0.7978845608028654 * (values + 0.044715 * values * values * values)))
    )


def rotary_tables(length, head):
    half = head // 2
    indices = jnp.arange(half, dtype=jnp.float32)
    freqs = jnp.exp(indices * (-2.0 * math.log(10000.0) / head))
    angles = jnp.arange(length, dtype=jnp.float32)[:, None] * freqs[None, :]
    return (jnp.cos(angles), jnp.sin(angles))


def rotate(values, tables):
    cosine = tables[0][:, None, :]
    sine = tables[1][:, None, :]
    half = values.shape[-1] // 2
    first = values[..., :half]
    second = values[..., half:]
    return jnp.concatenate(
        [first * cosine - second * sine, second * cosine + first * sine], axis=-1
    )


def unrotate(values, tables):
    cosine = tables[0][:, None, :]
    sine = tables[1][:, None, :]
    half = values.shape[-1] // 2
    first = values[..., :half]
    second = values[..., half:]
    return jnp.concatenate(
        [first * cosine + second * sine, second * cosine - first * sine], axis=-1
    )


def contract(left, right):
    return jnp.einsum("ri,rj->ij", left, right, preferred_element_type=jnp.float32)


def against(left, right):
    return jnp.einsum("rj,ij->ri", left, right, preferred_element_type=jnp.float32)


def norm_back(grad_normed, unit, scale, gain):
    scaled = grad_normed * gain.astype(jnp.float32)
    return scale * (scaled - unit * jnp.mean(scaled * unit, axis=1, keepdims=True))


def forward(frame_rows, skip_rows, weights, allowed, tables):
    w_skip, b_skip, gain_one, w_qkv, w_out, gain_two, w_up, b_up, w_down, b_down = weights
    length = frame_rows.shape[0]
    width = frame_rows.shape[1]
    joined = jnp.concatenate([frame_rows, skip_rows], axis=1)
    hidden = jnp.dot(joined, w_skip, preferred_element_type=jnp.float32) + b_skip.astype(
        jnp.float32
    )
    scale_one = lax.rsqrt(jnp.mean(hidden * hidden, axis=1, keepdims=True) + EPSILON)
    unit_one = hidden * scale_one
    normed_one = (unit_one * gain_one.astype(jnp.float32)).astype(jnp.bfloat16)
    mixed = jnp.dot(normed_one, w_qkv, preferred_element_type=jnp.float32)
    layout = (length, HEADS, HEAD)
    query = rotate(mixed[:, :width].reshape(layout), tables).astype(jnp.bfloat16)
    keys = rotate(mixed[:, width : 2 * width].reshape(layout), tables).astype(jnp.bfloat16)
    values = mixed[:, 2 * width :].reshape(layout).astype(jnp.bfloat16)
    scores = jnp.einsum("qhe,khe->hqk", query, keys, preferred_element_type=jnp.float32) * HEAD ** (
        -0.5
    )
    masked = jnp.where(allowed[None], scores, -1e30)
    highest = jnp.max(masked, axis=2, keepdims=True)
    exponent = jnp.exp(masked - highest)
    probs = exponent / jnp.sum(exponent, axis=2, keepdims=True)
    probs_low = probs.astype(jnp.bfloat16)
    attended = jnp.einsum("hqk,khe->qhe", probs_low, values, preferred_element_type=jnp.float32)
    attended = attended.reshape(length, width).astype(jnp.bfloat16)
    middle = hidden + jnp.dot(attended, w_out, preferred_element_type=jnp.float32)
    scale_two = lax.rsqrt(jnp.mean(middle * middle, axis=1, keepdims=True) + EPSILON)
    unit_two = middle * scale_two
    normed_two = (unit_two * gain_two.astype(jnp.float32)).astype(jnp.bfloat16)
    inner = jnp.dot(normed_two, w_up, preferred_element_type=jnp.float32) + b_up.astype(jnp.float32)
    activated = gelu_tanh(inner).astype(jnp.bfloat16)
    result = middle + (
        jnp.dot(activated, w_down, preferred_element_type=jnp.float32) + b_down.astype(jnp.float32)
    )
    saved = (
        joined,
        scale_one,
        unit_one,
        normed_one,
        query,
        keys,
        values,
        probs,
        probs_low,
        attended,
        scale_two,
        unit_two,
        normed_two,
        inner,
        activated,
    )
    return (result, saved)


def backward(grad_out, weights, saved, tables):
    w_skip, b_skip, gain_one, w_qkv, w_out, gain_two, w_up, b_up, w_down, b_down = weights
    (
        joined,
        scale_one,
        unit_one,
        normed_one,
        query,
        keys,
        values,
        probs,
        probs_low,
        attended,
        scale_two,
        unit_two,
        normed_two,
        inner,
        activated,
    ) = saved
    length = grad_out.shape[0]
    width = grad_out.shape[1]
    b_down_grad = jnp.sum(grad_out, axis=0)
    grad_low = grad_out.astype(jnp.bfloat16)
    w_down_grad = contract(activated, grad_low)
    grad_activated = against(grad_low, w_down)
    gelu_pull = jax.vjp(gelu_tanh, inner)[1]
    grad_inner = gelu_pull(grad_activated)[0]
    b_up_grad = jnp.sum(grad_inner, axis=0)
    inner_low = grad_inner.astype(jnp.bfloat16)
    w_up_grad = contract(normed_two, inner_low)
    grad_normed_two = against(inner_low, w_up)
    gain_two_grad = jnp.sum(grad_normed_two * unit_two, axis=0)
    grad_middle = grad_out + norm_back(grad_normed_two, unit_two, scale_two, gain_two)
    middle_low = grad_middle.astype(jnp.bfloat16)
    w_out_grad = contract(attended, middle_low)
    grad_attended = against(middle_low, w_out).astype(jnp.bfloat16).reshape(length, HEADS, HEAD)
    grad_probs = jnp.einsum(
        "qhe,khe->hqk", grad_attended, values, preferred_element_type=jnp.float32
    )
    grad_value = jnp.einsum(
        "hqk,qhe->khe", probs_low, grad_attended, preferred_element_type=jnp.float32
    )
    grad_scores = probs * (grad_probs - jnp.sum(grad_probs * probs, axis=2, keepdims=True))
    scores_low = grad_scores.astype(jnp.bfloat16)
    grad_query = jnp.einsum(
        "hqk,khe->qhe", scores_low, keys, preferred_element_type=jnp.float32
    ) * HEAD ** (-0.5)
    grad_key = jnp.einsum(
        "hqk,qhe->khe", scores_low, query, preferred_element_type=jnp.float32
    ) * HEAD ** (-0.5)
    grad_mixed = jnp.concatenate(
        [
            unrotate(grad_query, tables).reshape(length, width),
            unrotate(grad_key, tables).reshape(length, width),
            grad_value.reshape(length, width),
        ],
        axis=1,
    ).astype(jnp.bfloat16)
    w_qkv_grad = contract(normed_one, grad_mixed)
    grad_normed_one = against(grad_mixed, w_qkv)
    gain_one_grad = jnp.sum(grad_normed_one * unit_one, axis=0)
    grad_hidden = grad_middle + norm_back(grad_normed_one, unit_one, scale_one, gain_one)
    b_skip_grad = jnp.sum(grad_hidden, axis=0)
    hidden_low = grad_hidden.astype(jnp.bfloat16)
    w_skip_grad = contract(joined, hidden_low)
    grad_joined = against(hidden_low, w_skip)
    grads = (
        w_skip_grad,
        b_skip_grad,
        gain_one_grad,
        w_qkv_grad,
        w_out_grad,
        gain_two_grad,
        w_up_grad,
        b_up_grad,
        w_down_grad,
        b_down_grad,
    )
    return (grad_joined[:, :width], grad_joined[:, width:], grads)


def on_device(
    frames,
    skip,
    cotangent,
    segment_ids,
    row_lengths,
    w_skip,
    b_skip,
    gain_one,
    w_qkv,
    w_out,
    gain_two,
    w_up,
    b_up,
    w_down,
    b_down,
):
    micro_count = frames.shape[0]
    length = frames.shape[2]
    tables = rotary_tables(length, HEAD)
    positions = jnp.arange(length)
    diagonal = positions[:, None] == positions[None, :]
    results = []
    frame_grads = []
    skip_grads = []
    totals = None
    for micro in range(micro_count):
        gathered = (
            lax.all_gather(w_skip, ("dp", "fsdp"), axis=0, tiled=True),
            lax.all_gather(b_skip, ("dp", "fsdp"), axis=0, tiled=True),
            lax.all_gather(gain_one, ("dp", "fsdp"), axis=0, tiled=True),
            lax.all_gather(w_qkv, ("dp", "fsdp"), axis=0, tiled=True),
            lax.all_gather(w_out, ("dp", "fsdp"), axis=0, tiled=True),
            lax.all_gather(gain_two, ("dp", "fsdp"), axis=0, tiled=True),
            lax.all_gather(w_up, ("dp", "fsdp"), axis=0, tiled=True),
            lax.all_gather(b_up, ("dp", "fsdp"), axis=0, tiled=True),
            lax.all_gather(w_down, ("dp", "fsdp"), axis=0, tiled=True),
            lax.all_gather(b_down, ("dp", "fsdp"), axis=0, tiled=True),
        )
        segments = segment_ids[micro, 0]
        valid = positions[None, :] < row_lengths[micro, 0]
        allowed = (segments[:, None] == segments[None, :]) & valid | diagonal
        result, saved = forward(frames[micro, 0], skip[micro, 0], gathered, allowed, tables)
        results.append(result.astype(jnp.bfloat16))
        reused = (
            lax.all_gather(w_skip, ("dp", "fsdp"), axis=0, tiled=True),
            lax.all_gather(b_skip, ("dp", "fsdp"), axis=0, tiled=True),
            lax.all_gather(gain_one, ("dp", "fsdp"), axis=0, tiled=True),
            lax.all_gather(w_qkv, ("dp", "fsdp"), axis=0, tiled=True),
            lax.all_gather(w_out, ("dp", "fsdp"), axis=0, tiled=True),
            lax.all_gather(gain_two, ("dp", "fsdp"), axis=0, tiled=True),
            lax.all_gather(w_up, ("dp", "fsdp"), axis=0, tiled=True),
            lax.all_gather(b_up, ("dp", "fsdp"), axis=0, tiled=True),
            lax.all_gather(w_down, ("dp", "fsdp"), axis=0, tiled=True),
            lax.all_gather(b_down, ("dp", "fsdp"), axis=0, tiled=True),
        )
        frame_grad, skip_grad, grads = backward(
            cotangent[micro, 0].astype(jnp.float32), reused, saved, tables
        )
        frame_grads.append(frame_grad)
        skip_grads.append(skip_grad)
        shares = (
            lax.psum_scatter(grads[0], ("dp", "fsdp"), scatter_dimension=0, tiled=True),
            lax.psum_scatter(grads[1], ("dp", "fsdp"), scatter_dimension=0, tiled=True),
            lax.psum_scatter(grads[2], ("dp", "fsdp"), scatter_dimension=0, tiled=True),
            lax.psum_scatter(grads[3], ("dp", "fsdp"), scatter_dimension=0, tiled=True),
            lax.psum_scatter(grads[4], ("dp", "fsdp"), scatter_dimension=0, tiled=True),
            lax.psum_scatter(grads[5], ("dp", "fsdp"), scatter_dimension=0, tiled=True),
            lax.psum_scatter(grads[6], ("dp", "fsdp"), scatter_dimension=0, tiled=True),
            lax.psum_scatter(grads[7], ("dp", "fsdp"), scatter_dimension=0, tiled=True),
            lax.psum_scatter(grads[8], ("dp", "fsdp"), scatter_dimension=0, tiled=True),
            lax.psum_scatter(grads[9], ("dp", "fsdp"), scatter_dimension=0, tiled=True),
        )
        totals = (
            shares
            if totals is None
            else tuple((total + addend for total, addend in zip(totals, shares)))
        )
    stacked = jnp.stack(results)[:, None]
    frames_out = jnp.stack(frame_grads)[:, None]
    skip_out = jnp.stack(skip_grads)[:, None]
    return (
        stacked,
        frames_out,
        skip_out,
        totals[0],
        totals[1],
        totals[2],
        totals[3],
        totals[4],
        totals[5],
        totals[6],
        totals[7],
        totals[8],
        totals[9],
    )


def solution(mesh):
    return jax.shard_map(
        on_device,
        mesh=mesh,
        in_specs=(
            P(None, ("dp", "fsdp"), None, None),
            P(None, ("dp", "fsdp"), None, None),
            P(None, ("dp", "fsdp"), None, None),
            P(None, ("dp", "fsdp"), None),
            P(None, ("dp", "fsdp")),
            P(("dp", "fsdp"), None),
            P(("dp", "fsdp")),
            P(("dp", "fsdp")),
            P(("dp", "fsdp"), None),
            P(("dp", "fsdp"), None),
            P(("dp", "fsdp")),
            P(("dp", "fsdp"), None),
            P(("dp", "fsdp")),
            P(("dp", "fsdp"), None),
            P(("dp", "fsdp")),
        ),
        out_specs=(
            P(None, ("dp", "fsdp"), None, None),
            P(None, ("dp", "fsdp"), None, None),
            P(None, ("dp", "fsdp"), None, None),
            P(("dp", "fsdp"), None),
            P(("dp", "fsdp")),
            P(("dp", "fsdp")),
            P(("dp", "fsdp"), None),
            P(("dp", "fsdp"), None),
            P(("dp", "fsdp")),
            P(("dp", "fsdp"), None),
            P(("dp", "fsdp")),
            P(("dp", "fsdp"), None),
            P(("dp", "fsdp")),
        ),
        check_vma=False,
    )
```

profile of v0, /device:TPU:0, one launch (start us, length us, event | category | flops | bytes accessed | tf_op | source)
XLA Modules:
  0.0 1241.7 jit_solution(7571645208949470823)
XLA Ops:
  14.0 42.1 %all-reduce.10 = (bf16[1024]{0:T(1024)(128)(2,1)S(1)}, bf16[1024]{0:T(1024)(128)(2,1)S(1)}, bf16[1024]{0:T(1024)(128)(2,1)}, bf16[1024]{0:T(1024)(128)(2,1)S(1)}) all-reduce(bf16[1024]{0:T(1024)(128)(2,1)S(1)} %dynamic-update-slice, bf16[1024]{0:T(1024)(128)(2,1)S(1)} %dynamic-update-slice.1, ...), channel_id=1, replica_groups=mesh['dp'=8,'fsdp'=4] {'dp','fsdp'}, use_global_device_ids=true, to_apply=%add | all-reduce | flops 4096 | bytes 16384
  56.0 40.7 %all-gather = bf16[32,1,128]{2,1,0:T(2,128)(2,1)S(1)} all-gather(bf16[1,1,128]{2,1,0:T(2,128)(2,1)} %bitcast.168), channel_id=1, replica_groups=mesh['dp'=8,'fsdp'=4] {'dp','fsdp'}, dimensions={0}, use_global_device_ids=true | all-gather | bytes 8448 | tf_op jit(solution)/shard_map/all_gather | solution.py:237
  101.8 1.9 slice_bitcast_fusion.6
  103.8 4.3 multiply_reduce_fusion.11
  109.5 37.3 %all-gather.9.cloned.1.call-done = bf16[1024,3072]{1,0:T(8,128)(2,1)} async-done(((bf16[32,3072]{1,0:T(8,128)(2,1)}), bf16[1024,3072]{1,0:T(8,128)(2,1)}) %all-gather.9.cloned.1.call-update) | async-done | bytes 6291472 | tf_op jit(solution)/shard_map/all_gather | solution.py:233
  146.8 4.6 fusion.106
  154.1 4.7 fusion.105
  162.8 3.1 fusion.110
  165.9 2.5 copy.77
  168.4 2.5 copy.78
  170.9 2.0 copy.72
  173.0 3.4 subtract_convert_fusion.7
  176.3 4.6 fusion.113
  181.0 2.7 convolution_convert_fusion.4
  183.7 20.9 %all-gather.11.cloned.1.call-done = bf16[1024,1024]{1,0:T(8,128)(2,1)} async-done(((bf16[32,1024]{1,0:T(8,128)(2,1)}), bf16[1024,1024]{1,0:T(8,128)(2,1)}) %all-gather.11.cloned.1.call-update) | async-done | bytes 2097168 | tf_op jit(solution)/shard_map/all_gather | solution.py:234
  204.6 2.4 multiply_reduce_fusion.10
  207.6 5.3 fusion.114
  213.0 3.1 convolution_convert_fusion.5
  218.3 65.4 %all-gather.13.cloned.1.call-done = bf16[1024,4096]{1,0:T(8,128)(2,1)} async-done(((bf16[32,4096]{1,0:T(8,128)(2,1)}), bf16[1024,4096]{1,0:T(8,128)(2,1)}) %all-gather.13.cloned.1.call-update) | async-done | bytes 8388624 | tf_op jit(solution)/shard_map/all_gather | solution.py:236
  283.6 7.8 convolution_add_fusion.3
  291.4 71.0 %all-gather.15.cloned.1.call-done = bf16[4096,1024]{1,0:T(8,128)(2,1)} async-done(((bf16[128,1024]{1,0:T(8,128)(2,1)}), bf16[4096,1024]{1,0:T(8,128)(2,1)}) %all-gather.15.cloned.1.call-update) | async-done | bytes 8388624 | tf_op jit(solution)/shard_map/all_gather | solution.py:238
  362.4 9.4 fusion.116
  371.8 2.6 fusion.31
  374.5 5.9 convolution_add_fusion.4
  380.5 6.4 fusion.115
  386.9 7.2 multiply_reduce_fusion.3
  394.1 2.0 convert_reduce_fusion
  396.2 2.8 fusion.72
  400.5 2.0 copy.80
  402.6 5.3 multiply_reduce_fusion.1
  410.7 5.3 convolution_add_fusion.6
  416.3 4.4 multiply_convert_fusion.1
  431.8 2.0 multiply_reduce_fusion.5
  435.4 2.3 fusion.108
  439.4 4.8 convolution_add_fusion.5
  444.3 3.5 fusion.43
  447.8 6.5 convolution_add_fusion.2
  455.6 4.1 fusion.33
  459.7 9.9 convolution_add_fusion.1
  469.9 11.1 fusion.50
  481.0 11.0 convolution_add_fusion
  492.8 40.3 %all-reduce.9 = (f32[1024]{0:T(1024)S(1)}, f32[1024]{0:T(1024)S(1)}, f32[1024]{0:T(1024)S(1)}, f32[4096]{0:T(1024)S(1)}, f32[1024]{0:T(1024)S(1)}) all-reduce(f32[1024]{0:T(1024)S(1)} %add.254, f32[1024]{0:T(1024)S(1)} %add.255, f32[1024]{0:T(1024)S(1)} %add.258, ...), channel_id=13, replica_groups=mesh['dp'=8,'fsdp'=4] {'dp','fsdp'}, use_global_device_ids=true, to_apply=%region_17.18.clone | all-reduce | flops 8192 | bytes 65536
  536.0 7.6 fusion.28
  543.6 6.3 fusion.29
  557.1 146.8 %reduce-scatter.6.cloned.1.call-done = f32[64,1024]{1,0:T(8,128)} async-done(((f32[2048,1024]{1,0:T(8,128)}), f32[64,1024]{1,0:T(8,128)}) %reduce-scatter.6.cloned.1.call-update) | async-done | bytes 262160 | tf_op jit(solution)/shard_map/reduce_scatter | solution.py:264
  703.9 158.2 %reduce-scatter.8.cloned.1.call-done = f32[32,3072]{1,0:T(8,128)} async-done(((f32[1024,3072]{1,0:T(8,128)}), f32[32,3072]{1,0:T(8,128)}) %reduce-scatter.8.cloned.1.call-update) | async-done | bytes 393232 | tf_op jit(solution)/shard_map/reduce_scatter | solution.py:267
  862.1 185.0 %reduce-scatter.12.cloned.1.call-done = f32[32,4096]{1,0:T(8,128)} async-done(((f32[1024,4096]{1,0:T(8,128)}), f32[32,4096]{1,0:T(8,128)}) %reduce-scatter.12.cloned.1.call-update) | async-done | bytes 524304 | tf_op jit(solution)/shard_map/reduce_scatter | solution.py:270
  1047.1 187.2 %reduce-scatter.14.cloned.1.call-done = f32[128,1024]{1,0:T(8,128)} async-done(((f32[4096,1024]{1,0:T(8,128)}), f32[128,1024]{1,0:T(8,128)}) %reduce-scatter.14.cloned.1.call-update) | async-done | bytes 524304 | tf_op jit(solution)/shard_map/reduce_scatter | solution.py:272
  (246 shorter events, 53.7 us)
Async XLA Ops:
  7.2 96.6 %all-gather.7.cloned.1.call-start = ((), (), s32[]{:S(2)}) async-start(), calls=%async_computation.5 | async-start | bytes 4325376 | tf_op jit(solution)/shard_map/all_gather | solution.py:230
  7.9 138.9 %all-gather.9.cloned.1.call-start = ((), (), s32[]{:S(2)}) async-start(), calls=%async_computation.6 | async-start | bytes 6488064 | tf_op jit(solution)/shard_map/all_gather | solution.py:233
  8.7 195.9 %all-gather.11.cloned.1.call-start = ((), (), s32[]{:S(2)}) async-start(), calls=%async_computation.7 | async-start | bytes 2162688 | tf_op jit(solution)/shard_map/all_gather | solution.py:234
  9.4 274.2 %all-gather.13.cloned.1.call-start = ((), (), s32[]{:S(2)}) async-start(), calls=%async_computation.8 | async-start | bytes 8650752 | tf_op jit(solution)/shard_map/all_gather | solution.py:236
  10.0 352.4 %all-gather.15.cloned.1.call-start = ((), (), s32[]{:S(2)}) async-start(), calls=%async_computation.9 | async-start | bytes 8650752 | tf_op jit(solution)/shard_map/all_gather | solution.py:238
  10.6 546.5 %reduce-scatter.10.cloned.1.call-start = ((), (), s32[]{:S(2)}) async-start(), calls=%async_computation.12 | async-start | bytes 4325376 | tf_op jit(solution)/shard_map/reduce_scatter | solution.py:268
  103.7 4.4 copy-start.31
  103.7 4.4 copy-start.33
  103.7 5.8 copy-start.35
  103.7 5.8 copy-start.37
  103.8 4.3 copy-start.69
  108.0 96.5 %copy-start.3 = (f32[256,1024]{1,0:T(8,128)}, f32[256,1024]{1,0:T(8,128)S(1)}, u32[]{:S(2)}) copy-start(f32[256,1024]{1,0:T(8,128)S(1)} %get-tuple-element.130) | copy-start | bytes 3145732
  109.5 44.6 %copy-start.12 = (f32[256,1024]{1,0:T(8,128)}, f32[256,1024]{1,0:T(8,128)S(1)}, u32[]{:S(2)}) copy-start(f32[256,1024]{1,0:T(8,128)S(1)} %get-tuple-element.132) | copy-start | bytes 3145732
  176.3 4.7 copy-start.55
  183.7 29.3 %copy-start.28 = (bf16[16,64,256]{2,1,0:T(8,128)(2,1)}, bf16[16,64,256]{2,1,0:T(8,128)(2,1)S(1)}, u32[]{:S(2)}) copy-start(bf16[16,64,256]{2,1,0:T(8,128)(2,1)S(1)} %convolution_convert_fusion.4) | copy-start | bytes 1572868
  183.7 23.9 %copy-start.44 = (bf16[256,16,32]{0,2,1:T(8,128)(2,1)S(1)}, bf16[256,16,32]{0,2,1:T(8,128)(2,1)}, u32[]{:S(2)}) copy-start(bf16[256,16,32]{0,2,1:T(8,128)(2,1)} %get-tuple-element.91) | copy-start | bytes 786436
  183.7 23.9 %copy-start.46 = (bf16[256,16,32]{0,2,1:T(8,128)(2,1)S(1)}, bf16[256,16,32]{0,2,1:T(8,128)(2,1)}, u32[]{:S(2)}) copy-start(bf16[256,16,32]{0,2,1:T(8,128)(2,1)} %get-tuple-element.92) | copy-start | bytes 786436
  207.0 179.9 %copy-start.1 = (f32[256,1024]{1,0:T(8,128)}, f32[256,1024]{1,0:T(8,128)S(1)}, u32[]{:S(2)}) copy-start(f32[256,1024]{1,0:T(8,128)S(1)} %get-tuple-element.136) | copy-start | bytes 3145732
  213.0 3.5 copy-start.13
  216.1 67.5 %copy-start.63 = (f32[256]{0:T(256)S(1)}, f32[256]{0:T(256)}, u32[]{:S(2)}) copy-start(f32[256]{0:T(256)} %add_rsqrt_fusion) | copy-start | bytes 3076
  216.1 67.5 %copy-start.66 = (f32[32,1,128]{2,1,0:T(1,128)S(1)}, f32[32,1,128]{2,1,0:T(1,128)}, u32[]{:S(2)}) copy-start(f32[32,1,128]{2,1,0:T(1,128)} %convert_element_type.159) | copy-start | bytes 49156
  362.4 9.4 copy-start.68
  371.8 8.6 slice-start
  374.5 6.0 copy-start.15
  374.5 6.0 slice-start.1
  380.5 6.5 copy-start.10
  386.9 7.2 copy-start.25
  396.2 6.4 copy-start.62
  410.7 11.3 copy-start.57
  416.0 287.9 %reduce-scatter.6.cloned.1.call-start = ((), (), s32[]{:S(2)}) async-start(), calls=%async_computation.10 | async-start | bytes 8650752 | tf_op jit(solution)/shard_map/reduce_scatter | solution.py:264
  416.2 4.4 copy-start.48
  416.2 4.4 copy-start.49
  416.3 4.9 copy-start.45
  416.3 4.9 copy-start.47
  426.1 4.4 slice-start.2
  427.0 7.7 copy-start.20
  429.0 5.7 copy-start.22
  429.7 4.1 copy-start.54
  444.2 3.5 copy-start.21
  444.3 417.9 %reduce-scatter.8.cloned.1.call-start = ((), (), s32[]{:S(2)}) async-start(), calls=%async_computation.11 | async-start | bytes 12976128 | tf_op jit(solution)/shard_map/reduce_scatter | solution.py:267
  454.3 5.3 copy-start.2
  454.4 592.8 %reduce-scatter.12.cloned.1.call-start = ((), (), s32[]{:S(2)}) async-start(), calls=%async_computation.13 | async-start | bytes 17301504 | tf_op jit(solution)/shard_map/reduce_scatter | solution.py:270
  469.6 764.8 %reduce-scatter.14.cloned.1.call-start = ((), (), s32[]{:S(2)}) async-start(), calls=%async_computation.14 | async-start | bytes 17301504 | tf_op jit(solution)/shard_map/reduce_scatter | solution.py:272
  469.9 11.1 copy-start.5
  469.9 11.1 copy-start.16
  536.0 7.6 copy-start.11
  543.6 7.4 copy-start.27
  543.6 7.4 copy-start.70
  (37 other events, 77.2 us)
Sparse Core Ops, SparseCore 0:
  10.9 64.9 all-gather.6
  78.7 68.0 all-gather.8
  149.7 54.8 all-gather.10
  207.3 76.2 all-gather.12
  286.3 76.0 all-gather.14
  416.1 139.7 reduce-scatter.9
  558.8 145.0 reduce-scatter.5
  710.5 151.5 reduce-scatter.7
  865.1 182.0 reduce-scatter.11
  1050.0 184.3 reduce-scatter.13
where the time goes:
time: 1250 us; the launch traced here: 1240 us
  waiting for transfers between devices  875 us (70%)
  matrix products  168 us (13%)
  blocking collectives  123 us (10%)
  local copies, waits for them, and re-layouts  39 us (3%)
  other arithmetic  19.5 us (2%)
  between operations  15.7 us (1%)
    reduce_scatter x1, waiting for transfers between devices, on_device(): lax.psum_scatter(grads[8], ('dp', 'fsdp'), scatter_dimension=0, tiled=True)  187 us
    reduce_scatter x1, waiting for transfers between devices, on_device(): lax.psum_scatter(grads[6], ('dp', 'fsdp'), scatter_dimension=0, tiled=True)  185 us
    reduce_scatter x1, waiting for transfers between devices, on_device(): lax.psum_scatter(grads[3], ('dp', 'fsdp'), scatter_dimension=0, tiled=True)  158 us
    reduce_scatter x1, waiting for transfers between devices, on_device(): lax.psum_scatter(grads[0], ('dp', 'fsdp'), scatter_dimension=0, tiled=True)  147 us
    unnamed x2, blocking collectives  82.3 us
    all_gather x1, waiting for transfers between devices, on_device(): lax.all_gather(w_down, ('dp', 'fsdp'), axis=0, tiled=True)  71 us
    all_gather x1, waiting for transfers between devices, on_device(): lax.all_gather(w_up, ('dp', 'fsdp'), axis=0, tiled=True)  65.4 us
    dot_general x10, matrix products, contract(): jnp.einsum('ri,rj->ij', left, right, preferred_element_type=jnp.float32)  60.2 us
  transfers between devices with their start and end apart: 10, of which 8 were waited for; matrix products, arithmetic and copies ran while one was open for 13% of the time, Pallas kernels for 0%

commit v1 on v0

v1 whole, which is shorter than its diff:
```python
import functools
import math

import jax
import jax.numpy as jnp
from jax import lax
from jax.experimental import pallas as pl
from jax.experimental.pallas import tpu as pltpu
from jax.sharding import PartitionSpec as P

HEADS = 16
HEAD = 64
EPSILON = 1e-06
AXES = ("dp", "fsdp")
F32 = jnp.float32
BF16 = jnp.bfloat16


def dot(left, right, kind=F32):
    return jnp.dot(left, right, preferred_element_type=F32).astype(kind)


def against(left, right):
    return lax.dot_general(left, right, (((1,), (1,)), ((), ())), preferred_element_type=F32)


def contract(left, right):
    return lax.dot_general(left, right, (((0,), (0,)), ((), ())), preferred_element_type=F32)


def wide_tables(length):
    half = HEAD // 2
    indices = jnp.arange(half, dtype=F32)
    freqs = jnp.exp(indices * (-2.0 * math.log(10000.0) / HEAD))
    angles = jnp.arange(length, dtype=F32)[:, None] * freqs[None, :]
    cosine, sine = jnp.cos(angles), jnp.sin(angles)
    return (
        jnp.concatenate([cosine] * 4, axis=1),
        jnp.concatenate([-sine, sine, -sine, sine], axis=1),
    )


def swap_halves(values):
    half = HEAD // 2
    lane = lax.broadcasted_iota(jnp.int32, values.shape, 1)
    ahead = pltpu.roll(values, 2 * HEAD - half, 1)
    behind = pltpu.roll(values, half, 1)
    return jnp.where(lax.rem(lane, HEAD) < half, ahead, behind)


def allowed_of(column_ref, row_ref):
    length = row_ref.shape[-1]
    rows = lax.broadcasted_iota(jnp.int32, (length, length), 0)
    columns = lax.broadcasted_iota(jnp.int32, (length, length), 1)
    return (column_ref[0] == row_ref[0]) | (rows == columns)


def head_part(values, which):
    lane = lax.broadcasted_iota(jnp.int32, values.shape, 1)
    return jnp.where((lane >= HEAD) == (which == 1), values, jnp.zeros_like(values))


def attend_kernel(q_ref, k_ref, v_ref, cos_ref, sin_ref, column_ref, row_ref, qo_ref, ko_ref, vo_ref, a_ref, lse_ref):
    pair = pl.program_id(1)
    cosine, sine = cos_ref[...], sin_ref[...]
    raw_q, raw_k = q_ref[...], k_ref[...]
    query = (raw_q * cosine + swap_halves(raw_q) * sine).astype(BF16)
    key = (raw_k * cosine + swap_halves(raw_k) * sine).astype(BF16)
    value = v_ref[...].astype(BF16)
    qo_ref[...] = query
    ko_ref[...] = key
    vo_ref[...] = value
    allowed = allowed_of(column_ref, row_ref)
    total = jnp.zeros(value.shape, F32)
    lane = lax.broadcasted_iota(jnp.int32, lse_ref.shape, 1)

    @pl.when(pair == 0)
    def _():
        lse_ref[...] = jnp.zeros_like(lse_ref)

    marks = lse_ref[...]
    for which in range(2):
        scores = against(head_part(query, which), key) * HEAD ** (-0.5)
        masked = jnp.where(allowed, scores, -1e30)
        highest = jnp.max(masked, axis=1, keepdims=True)
        exponent = jnp.exp(masked - highest)
        summed = jnp.sum(exponent, axis=1, keepdims=True)
        probs = (exponent / summed).astype(BF16)
        total += dot(probs, head_part(value, which))
        marks = jnp.where(lane == 2 * pair + which, highest + jnp.log(summed), marks)
    lse_ref[...] = marks
    a_ref[...] = total.astype(BF16)


def attend(mixed, tables, column, row, rows, length):
    width = HEADS * HEAD
    pairs = HEADS // 2
    wide = 2 * HEAD
    place = lambda shift: pl.BlockSpec((length, wide), lambda r, p, s=shift: (r, p + s))
    table = pl.BlockSpec((length, wide), lambda r, p: (0, 0))
    narrow = jax.ShapeDtypeStruct((rows * length, width), BF16)
    return pl.pallas_call(
        attend_kernel,
        grid=(rows, pairs),
        in_specs=[
            place(0),
            place(pairs),
            place(2 * pairs),
            table,
            table,
            pl.BlockSpec((1, length, 1), lambda r, p: (r, 0, 0)),
            pl.BlockSpec((1, 1, length), lambda r, p: (r, 0, 0)),
        ],
        out_specs=[place(0)] * 4 + [pl.BlockSpec((length, wide), lambda r, p: (r, 0))],
        out_shape=[narrow] * 4 + [jax.ShapeDtypeStruct((rows * length, wide), F32)],
        cost_estimate=pl.CostEstimate(flops=rows * HEADS * length * length * 512, bytes_accessed=rows * length * width * 24, transcendentals=rows * HEADS * length * length),
    )(mixed, mixed, mixed, *tables, column, row)


def attend_back_kernel(q_ref, k_ref, v_ref, g_ref, lse_ref, cos_ref, sin_ref, column_ref, row_ref, gq_ref, gk_ref, gv_ref):
    pair = pl.program_id(1)
    cosine, sine = cos_ref[...], sin_ref[...]
    query, key, value, grad = q_ref[...], k_ref[...], v_ref[...], g_ref[...]
    allowed = allowed_of(column_ref, row_ref)
    lse = lse_ref[...]
    lane = lax.broadcasted_iota(jnp.int32, lse.shape, 1)
    scale = HEAD ** (-0.5)
    grad_q = jnp.zeros(query.shape, F32)
    grad_k = jnp.zeros(query.shape, F32)
    grad_v = jnp.zeros(query.shape, F32)
    for which in range(2):
        own_query = head_part(query, which)
        own_grad = head_part(grad, which)
        mark = jnp.sum(jnp.where(lane == 2 * pair + which, lse, 0.0), axis=1, keepdims=True)
        scores = against(own_query, key) * scale
        probs = jnp.exp(jnp.where(allowed, scores, -1e30) - mark)
        grad_probs = against(own_grad, value)
        inside = jnp.sum(grad_probs * probs, axis=1, keepdims=True)
        grad_scores = (probs * (grad_probs - inside)).astype(BF16)
        grad_v += contract(probs.astype(BF16), own_grad)
        grad_q += dot(grad_scores, head_part(key, which))
        grad_k += contract(grad_scores, own_query)
    grad_q = grad_q * scale
    grad_k = grad_k * scale
    gq_ref[...] = (grad_q * cosine - swap_halves(grad_q) * sine).astype(BF16)
    gk_ref[...] = (grad_k * cosine - swap_halves(grad_k) * sine).astype(BF16)
    gv_ref[...] = grad_v.astype(BF16)


def attend_back(query, key, value, grad, lse, tables, column, row, rows, length):
    width = HEADS * HEAD
    pairs = HEADS // 2
    wide = 2 * HEAD
    place = pl.BlockSpec((length, wide), lambda r, p: (r, p))
    table = pl.BlockSpec((length, wide), lambda r, p: (0, 0))
    narrow = jax.ShapeDtypeStruct((rows * length, width), BF16)
    return pl.pallas_call(
        attend_back_kernel,
        grid=(rows, pairs),
        in_specs=[place] * 4
        + [
            pl.BlockSpec((length, wide), lambda r, p: (r, 0)),
            table,
            table,
            pl.BlockSpec((1, length, 1), lambda r, p: (r, 0, 0)),
            pl.BlockSpec((1, 1, length), lambda r, p: (r, 0, 0)),
        ],
        out_specs=[place] * 3,
        out_shape=[narrow] * 3,
        cost_estimate=pl.CostEstimate(flops=rows * HEADS * length * length * 1280, bytes_accessed=rows * length * width * 14, transcendentals=rows * HEADS * length * length),
    )(query, key, value, grad, lse, *tables, column, row)


def gelu_parts(values):
    cube = values * values
    arch = jnp.tanh(0.7978845608028654 * (values + 0.044715 * values * cube))
    slope = 0.5 * (1.0 + arch) + 0.5 * values * (1.0 - arch * arch) * (0.7978845608028654 * (1.0 + 3.0 * 0.044715 * cube))
    return 0.5 * values * (1.0 + arch), slope


def norm_back(grad_normed, unit, scale, gain):
    scaled = grad_normed * gain
    return scale * (scaled - unit * jnp.mean(scaled * unit, axis=1, keepdims=True))


def pairs_of(move):
    pairs = []
    for z in range(4):
        for y in range(2):
            for x in range(2):
                for c in range(2):
                    there = move(z, y, x, c)
                    if there is not None:
                        source = ((z * 2 + y) * 2 + x) * 2 + c
                        target = ((there[0] * 2 + there[1]) * 2 + there[2]) * 2 + there[3]
                        pairs.append((source, target))
    return pairs


OTHER_CORE = pairs_of(lambda z, y, x, c: (z, y, x, 1 - c))
FIRST = pairs_of(lambda z, y, x, c: (z, 1 - y, x, c) if c == 0 else (z, y, 1 - x, c))
SECOND = pairs_of(lambda z, y, x, c: (z, y, 1 - x, c) if c == 0 else (z, 1 - y, x, c))
INWARD = pairs_of(lambda z, y, x, c: {0: (1, y, x, c), 3: (2, y, x, c)}.get(z))
MIDDLE = pairs_of(lambda z, y, x, c: {1: (2, y, x, c), 2: (1, y, x, c)}.get(z))
NEAR = pairs_of(lambda z, y, x, c: (z ^ 1, y, x, c))
Z_ORDER = ((3, 2, 1, 0), (3, 2, 0, 1), (0, 1, 3, 2), (0, 1, 2, 3))


def send(values, pairs):
    return lax.ppermute(values, AXES, pairs)


def block_order(place, late_plane, core):
    z, y, x = place
    levels = jnp.asarray(Z_ORDER, jnp.int32)[z]
    own_first = jnp.where(core == 0, y, x)
    own_second = jnp.where(core == 0, x, y)
    index = jnp.arange(16)
    if late_plane:
        first, slot, second = index // 8, index // 2 % 4, index % 2
    else:
        first, second, slot = index // 8, index // 4 % 2, index % 4
    level = jnp.sum(jnp.where(slot[:, None] == jnp.arange(4)[None, :], levels[None, :], 0), axis=1)
    first = jnp.where(first == 1, own_first, 1 - own_first)
    second = jnp.where(second == 1, own_second, 1 - own_second)
    at_y = jnp.where(core == 0, first, second)
    at_x = jnp.where(core == 0, second, first)
    return ((level * 2 + at_y) * 2 + at_x) * 2 + core


def both_orders(place, core, late_plane):
    return jnp.concatenate([block_order(place, late_plane, 1 - core), block_order(place, late_plane, core)])


def plus(left, right, kind=BF16):
    return (left.astype(F32) + right.astype(F32)).astype(kind)


def reduce(values, late_plane):
    half = values.shape[0] // 2
    kept = plus(values[half:], send(values[:half], FIRST))
    if not late_plane:
        half //= 2
        kept = plus(kept[half:], send(kept[:half], SECOND))
    half //= 2
    far = plus(kept[:half], send(kept[:half], INWARD))
    near = plus(kept[half:], send(far, MIDDLE))
    half //= 2
    if not late_plane:
        return plus(near[half:], send(near[:half], NEAR), F32)
    kept = plus(near[half:], send(near[:half], NEAR))
    half //= 2
    return plus(kept[half:], send(kept[:half], SECOND), F32)


def picked(values, order):
    columns = values.shape[1]
    block = columns // 32
    column = jnp.arange(columns)
    source = jnp.repeat(order, block) * block + column % block
    choice = (column[:, None] == source[None, :]).astype(BF16)
    return dot(values, choice, BF16)


def copy_kernel(order_ref, in_ref, out_ref):
    out_ref[...] = in_ref[...]


def picked_wide(values, order):
    rows, columns = values.shape
    block = columns // 32
    return pl.pallas_call(
        copy_kernel,
        grid_spec=pltpu.PrefetchScalarGridSpec(
            num_scalar_prefetch=1,
            grid=(32,),
            in_specs=[pl.BlockSpec((rows, block), lambda i, order: (0, order[i]))],
            out_specs=pl.BlockSpec((rows, block), lambda i, order: (0, i)),
        ),
        out_shape=jax.ShapeDtypeStruct(values.shape, values.dtype),
        cost_estimate=pl.CostEstimate(flops=0, bytes_accessed=4 * rows * columns, transcendentals=0),
    )(order, values)


def paired(values):
    half = values.shape[1] // 2
    return jnp.concatenate([values[:, half:], send(values[:, :half], OTHER_CORE)])


def with_other(values):
    return jnp.concatenate([values, send(values, OTHER_CORE)])


def on_device(
    known,
    frames,
    skip,
    cotangent,
    segment_ids,
    row_lengths,
    w_skip,
    b_skip,
    gain_one,
    w_qkv,
    w_out,
    gain_two,
    w_up,
    b_up,
    w_down,
    b_down,
):
    micro, rows, length, width = frames.shape
    count = micro * rows
    tokens = count * length
    devices = width // gain_one.shape[0]
    hidden_width = w_up.shape[1]

    vectors = jnp.concatenate([b_skip, gain_one, gain_two, b_down, b_up])
    part = w_skip.shape[0]
    lines = -(-vectors.shape[0] // width)
    lines = -(-lines // 8) * 8
    padded = jnp.pad(vectors, (0, lines * width - vectors.shape[0])).reshape(lines, width)
    all_skip = lax.all_gather(jnp.concatenate([w_skip, padded]), AXES, axis=0, tiled=False)
    all_qkv = lax.all_gather(jnp.concatenate([w_qkv, w_out], axis=1), AXES, axis=0, tiled=True)
    all_up = lax.all_gather(w_up, AXES, axis=0, tiled=True)
    all_down = lax.all_gather(w_down, AXES, axis=0, tiled=True)
    full_skip = all_skip[:, :part].reshape(devices * part, width)
    flat = all_skip[:, part:].reshape(devices, lines * width)
    small = width // devices
    spread = lambda at, size: flat[:, at : at + size].reshape(1, devices * size).astype(F32)
    bias_skip, gain_1, gain_2, bias_down = (spread(i * small, small) for i in range(4))
    bias_up = spread(4 * small, hidden_width // devices)
    full_qkv = all_qkv[:, : 3 * width]
    full_out = all_qkv[:, 3 * width :]

    frames = frames.reshape(tokens, width)
    skip = skip.reshape(tokens, width)
    grad_low = cotangent.reshape(tokens, width)
    grad_out = grad_low.astype(F32)
    segments = segment_ids.reshape(count, length)
    lengths = row_lengths.reshape(count, 1)
    reach = jnp.where(jnp.arange(length)[None, :] < lengths, segments, -1)
    column, row = segments[:, :, None], reach[:, None, :]
    tables = wide_tables(length)

    joined = jnp.concatenate([frames, skip], axis=1)
    hidden = dot(joined, full_skip) + bias_skip
    scale_one = lax.rsqrt(jnp.mean(hidden * hidden, axis=1, keepdims=True) + EPSILON)
    unit_one = hidden * scale_one
    normed_one = (unit_one * gain_1).astype(BF16)
    mixed = dot(normed_one, full_qkv)
    query, key, value, attended, lse = attend(mixed, tables, column, row, count, length)
    middle = hidden + dot(attended, full_out)
    scale_two = lax.rsqrt(jnp.mean(middle * middle, axis=1, keepdims=True) + EPSILON)
    unit_two = middle * scale_two
    normed_two = (unit_two * gain_2).astype(BF16)
    inner = dot(normed_two, all_up) + bias_up
    activated, slope = gelu_parts(inner)
    activated = activated.astype(BF16)
    output = (middle + (dot(activated, all_down) + bias_down)).astype(BF16)

    grad_inner = against(grad_low, all_down) * slope
    inner_low = grad_inner.astype(BF16)
    grad_normed_two = against(inner_low, all_up)
    grad_middle = grad_out + norm_back(grad_normed_two, unit_two, scale_two, gain_2)
    middle_low = grad_middle.astype(BF16)
    grad_attended = against(middle_low, full_out).astype(BF16)
    grad_mixed = jnp.concatenate(attend_back(query, key, value, grad_attended, lse, tables, column, row, count, length), axis=1)
    grad_normed_one = against(grad_mixed, full_qkv)
    grad_hidden = grad_middle + norm_back(grad_normed_one, unit_one, scale_one, gain_1)
    hidden_low = grad_hidden.astype(BF16)
    grad_joined = against(hidden_low, full_skip)

    total = lambda values: jnp.sum(values, axis=0)
    vector_grads = (
        total(grad_hidden),
        total(grad_normed_one * unit_one),
        total(grad_normed_two * unit_two),
        total(grad_out),
        total(grad_inner),
    )

    if known:
        place = lax.axis_index("dp")
        at_x = lax.axis_index("fsdp")
        core = at_x % 2
        coords = (place // 2, place % 2, at_x // 2)
        late = both_orders(coords, core, True)
        early = both_orders(coords, core, False)
        g_down = contract(paired(picked_wide(activated, late)), with_other(grad_low)).astype(BF16)
        down_grad = reduce(g_down, True)
        g_up = contract(paired(picked(normed_two, late)), with_other(inner_low)).astype(BF16)
        up_grad = reduce(g_up, True)
        g_out = contract(paired(picked(attended, early)), with_other(middle_low)).astype(BF16)
        g_qkv = contract(paired(picked(normed_one, early)), with_other(grad_mixed)).astype(BF16)
        both_grad = reduce(jnp.concatenate([g_qkv, g_out], axis=1), False)
        qkv_grad, out_grad = both_grad[:, : 3 * width], both_grad[:, 3 * width :]
        g_skip = contract(paired(picked(joined, early)), with_other(hidden_low)).astype(BF16)
        by_block = jnp.concatenate([v.reshape(devices, -1) for v in vector_grads], axis=1)
        by_block = by_block + send(by_block, OTHER_CORE)
        choice = (early[16:, None] == jnp.arange(devices)[None, :]).astype(F32)
        by_block = jnp.dot(choice, by_block, precision=lax.Precision.HIGHEST).astype(BF16)
        by_block = jnp.pad(by_block, ((0, 0), (0, lines * width - by_block.shape[1])))
        g_last = jnp.concatenate([g_skip.reshape(16, part, width), by_block.reshape(16, lines, width)], axis=1)
        last = reduce(g_last.reshape(16 * (part + lines), width), False)
        skip_weight_grad = last[:part]
        line = last[part:].reshape(lines * width)
        shares = [line[i * small : (i + 1) * small] for i in range(4)]
        shares.append(line[4 * small : 4 * small + hidden_width // devices])
    else:
        scatter = lambda values: lax.psum_scatter(values, AXES, scatter_dimension=0, tiled=True)
        down_grad = scatter(contract(activated, grad_low))
        up_grad = scatter(contract(normed_two, inner_low))
        out_grad = scatter(contract(attended, middle_low))
        qkv_grad = scatter(contract(normed_one, grad_mixed))
        skip_weight_grad = scatter(contract(joined, hidden_low))
        shares = [scatter(v) for v in vector_grads]

    shape = (micro, rows, length, width)
    return (
        output.reshape(shape),
        grad_joined[:, :width].reshape(shape),
        grad_joined[:, width:].reshape(shape),
        skip_weight_grad,
        shares[0],
        shares[1],
        qkv_grad,
        out_grad,
        shares[2],
        up_grad,
        shares[4],
        down_grad,
        shares[3],
    )


def solution(mesh):
    known = mesh.shape["dp"] == 8 and mesh.shape["fsdp"] == 4
    tokens = P(None, AXES, None, None)
    weight = P(AXES, None)
    vector = P(AXES)
    return jax.shard_map(
        functools.partial(on_device, known),
        mesh=mesh,
        in_specs=(
            tokens,
            tokens,
            tokens,
            P(None, AXES, None),
            P(None, AXES),
            weight,
            vector,
            vector,
            weight,
            weight,
            vector,
            weight,
            vector,
            weight,
            vector,
        ),
        out_specs=(
            tokens,
            tokens,
            tokens,
            weight,
            vector,
            vector,
            weight,
            weight,
            vector,
            weight,
            vector,
            weight,
            vector,
        ),
        check_vma=False,
    )
```

time: 1250 us -> 637 us (0.51)
  waiting for transfers between devices: 875 us -> 320 us
  blocking collectives: 123 us -> 0 us
  starting transfers between devices: 0.82 us -> 64.1 us
  Pallas kernels: 0 us -> 61.4 us
  matrix products: 168 us -> 115 us
    reduce_scatter x5 -> x0, waiting for transfers between devices: 677 us -> none  [the longest x1 187 us: on_device(): lax.psum_scatter(grads[8], ('dp', 'fsdp'), scatter_dimension=0, tiled=True)]
    ppermute x0 -> x31, waiting for transfers between devices: none -> 92.4 us  [send(): return lax.ppermute(values, AXES, pairs)]
    unnamed x2 -> x0, blocking collectives: 82.3 us -> none
    ppermute x0 -> x31, starting transfers between devices: none -> 63.9 us  [send(): return lax.ppermute(values, AXES, pairs)]
    pallas_call x0 -> x3, Pallas kernels: none -> 61.4 us  [the longest x1 27.1 us: picked_wide(): pl.pallas_call(copy_kernel, grid_spec=pltpu.PrefetchScalarGridSpec(num_sc...]
    dot_general x40 -> x20, matrix products: 158 us -> 115 us  [the longest x9 51.1 us: dot(): return jnp.dot(left, right, preferred_element_type=F32).astype(kind)]
    all_gather x1 -> x0, blocking collectives: 40.7 us -> none  [on_device(): lax.all_gather(b_up, ('dp', 'fsdp'), axis=0, tiled=True)]
    all_gather x5 -> x4, waiting for transfers between devices: 195 us -> 226 us  [the longest x1 65.9 us: on_device(): all_down = lax.all_gather(w_down, AXES, axis=0, tiled=True)]
  transfers between devices with their start and end apart: 10 -> 35, of which waited for: 8 -> 16; matrix products, arithmetic and copies ran while one was open for 13% -> 25% of each run, Pallas kernels for 0% -> 10%
where the time goes in v1:
time: 637 us; the launch traced here: 627 us
  waiting for transfers between devices  320 us (50%)
  matrix products  115 us (18%)
  starting transfers between devices  64.1 us (10%)
  Pallas kernels  61.4 us (10%)
  local copies, waits for them, and re-layouts  32.1 us (5%)
  other arithmetic  19.7 us (3%)
  between operations  15 us (2%)
    ppermute x31, waiting for transfers between devices, send(): return lax.ppermute(values, AXES, pairs)  92.4 us
    all_gather x1, waiting for transfers between devices, on_device(): all_down = lax.all_gather(w_down, AXES, axis=0, tiled=True)  65.9 us
    ppermute x31, starting transfers between devices, send(): return lax.ppermute(values, AXES, pairs)  63.9 us
    all_gather x1, waiting for transfers between devices, on_device(): lax.all_gather(jnp.concatenate([w_qkv, w_out], axis=1), AXES, axis=0, til...  63.6 us
    dot_general x9, matrix products, dot(): return jnp.dot(left, right, preferred_element_type=F32).astype(kind)  51.1 us
    all_gather x1, waiting for transfers between devices, on_device(): lax.all_gather(jnp.concatenate([w_skip, padded]), AXES, axis=0, tiled=False)  49.7 us
    all_gather x1, waiting for transfers between devices, on_device(): all_up = lax.all_gather(w_up, AXES, axis=0, tiled=True)  47.1 us
    dot_general x5, matrix products, against(): lax.dot_general(left, right, (((1,), (1,)), ((), ())), preferred_element_...  36.8 us
  transfers between devices with their start and end apart: 35, of which 16 were waited for; matrix products, arithmetic and copies ran while one was open for 25% of the time, Pallas kernels for 10%

profile of v1, /device:TPU:0, one launch (start us, length us, event | category | flops | bytes accessed | tf_op | source)
XLA Modules:
  0.0 627.1 jit_solution(7252714253351887462)
XLA Ops:
  7.2 3.4 concatenate.67
  12.3 1.7 pad_maximum_fusion.5
  16.4 6.4 %fusion.30 = bf16[512,2048]{1,0:T(8,128)(2,1)S(1)} fusion(s32[2048]{0:T(1024)S(1)} %fusion.85, bf16[512,1024]{1,0:T(8,128)(2,1)} %bitcast.77, bf16[512,1024]{1,0:T(8,128)(2,1)} %bitcast.79), kind=kOutput, calls=%fused_computation.35 | convolution fusion | flops 4304404480 | bytes 4202496 | tf_op jit(solution)/shard_map/dot_general | solution.py:20
  29.0 49.7 %all-gather.12.cloned.1.call-done = bf16[2304,1024]{1,0:T(8,128)(2,1)} async-done(((bf16[72,1024]{1,0:T(8,128)(2,1)}), bf16[2304,1024]{1,0:T(8,128)(2,1)}) %all-gather.12.cloned.1.call-update) | async-done | bytes 4718608 | tf_op jit(solution)/shard_map/all_gather | solution.py:323
  79.9 5.0 slice.257
  86.3 5.3 multiply_reduce_fusion.5
  94.9 63.6 %all-gather.6.cloned.1.call-done = bf16[1024,4096]{1,0:T(8,128)(2,1)} async-done(((bf16[32,4096]{1,0:T(8,128)(2,1)}), bf16[1024,4096]{1,0:T(8,128)(2,1)}) %all-gather.6.cloned.1.call-update) | async-done | bytes 8388624 | tf_op jit(solution)/shard_map/all_gather | solution.py:324
  158.5 8.2 %fusion.15.q_ref.k_ref.v_ref = f32[512,3072]{1,0:T(8,128)} fusion(bf16[1024,4096]{1,0:T(8,128)(2,1)} %all-gather.6.cloned.1.call-done, f32[512,1024]{1,0:T(8,128)S(1)} %get-tuple-element.114, f32[1024]{0:T(1024)S(1)} %reshape.339, f32[512]{0:T(512)S(1)} %add_rsqrt_fusion.1, f32[1024]{0:T(1024)S(1)} %reshape.338), kind=kOutput, calls=%fused_computation.17 | convolution fusion | flops 3223322624 | bytes 14690304 | tf_op jit(solution)/shard_map/dot_general | solution.py:20
  166.7 17.1 %shard_map.285 = (bf16[512,1024]{1,0:T(8,128)(2,1)}, bf16[512,1024]{1,0:T(8,128)(2,1)}, bf16[512,1024]{1,0:T(8,128)(2,1)}, bf16[512,1024]{1,0:T(8,128)(2,1)}, f32[512,128]{1,0:T(8,128)}) custom-call(f32[512,3072]{1,0:T(8,128)} %fusion.15.q_ref.k_ref.v_ref, f32[512,3072]{1,0:T(8,128)} %fusion.15.q_ref.k_ref.v_ref, f32[512,3072]{1,0:T(8,128)} %fusion.15.q_ref.k_ref.v_ref, ...), custom_call_target="tpu_custom_call" | custom-call | flops 1073741824 | bytes 12582912 | tf_op jit(solution)/shard_map/pallas_call | solution.py:102
  183.9 4.0 multiply_reduce_fusion.4
  187.9 2.3 fusion.69
  190.2 47.1 %all-gather.8.cloned.1.call-done = bf16[1024,4096]{1,0:T(8,128)(2,1)} async-done(((bf16[32,4096]{1,0:T(8,128)(2,1)}), bf16[1024,4096]{1,0:T(8,128)(2,1)}) %all-gather.8.cloned.1.call-update) | async-done | bytes 8388624 | tf_op jit(solution)/shard_map/all_gather | solution.py:325
  237.4 12.9 %multiply_convert_fusion = (bf16[512,4096]{1,0:T(8,128)(2,1)}, f32[512,4096]{1,0:T(8,128)}) fusion(f32[4096]{0:T(1024)S(1)} %fusion.86, bf16[1024,4096]{1,0:T(8,128)(2,1)} %all-gather.8.cloned.1.call-done, f32[512,1024]{1,0:T(8,128)S(1)} %get-tuple-element.116, f32[1024]{0:T(1024)S(1)} %reshape.340, f32[512]{0:T(512)S(1)} %add_rsqrt_fusion), kind=kOutput, calls=%fused_computation.8 | convolution fusion | flops 4317511680 | bytes 23091200 | tf_op jit(solution)/shard_map/dot_general | solution.py:20
  250.3 65.9 %all-gather.10.cloned.1.call-done = bf16[4096,1024]{1,0:T(8,128)(2,1)} async-done(((bf16[128,1024]{1,0:T(8,128)(2,1)}), bf16[4096,1024]{1,0:T(8,128)(2,1)}) %all-gather.10.cloned.1.call-update) | async-done | bytes 8388624 | tf_op jit(solution)/shard_map/all_gather | solution.py:326
  316.2 15.2 %fusion.121 = (f32[4096]{0:T(1024)S(1)}, bf16[512,4096]{1,0:T(8,128)(2,1)}) fusion(f32[512,4096]{1,0:T(8,128)} %get-tuple-element.118, f32[4096]{0:T(1024)S(1)} %fusion.86, bf16[512,1024]{1,0:T(8,128)(2,1)S(1)} %bitcast.57, bf16[4096,1024]{1,0:T(8,128)(2,1)} %all-gather.10.cloned.1.call-done), kind=kOutput, calls=%fused_computation.224 | convolution fusion | flops 4336906240 | bytes 22052864 | tf_op jit(solution)/shard_map/dot_general | solution.py:24
  331.4 6.8 %multiply_reduce_fusion = (f32[1024]{0:T(1024)S(1)}, f32[512]{0:T(512)S(1)}, f32[512,1024]{1,0:T(8,128)S(1)}) fusion(f32[512,1024]{1,0:T(8,128)S(1)} %get-tuple-element.116, f32[512]{0:T(512)S(1)} %add_rsqrt_fusion, f32[1024]{0:T(1024)S(1)} %reshape.340, bf16[512,4096]{1,0:T(8,128)(2,1)} %get-tuple-element.79, bf16[1024,4096]{1,0:T(8,128)(2,1)S(1)} %copy-done.17), kind=kOutput, calls=%fused_computation.66 | convolution fusion | flops 4298111488 | bytes 16789504 | tf_op jit(solution)/shard_map/dot_general | solution.py:24
  338.2 1.6 fusion.119
  340.1 4.2 fusion.61.g_ref
  344.3 17.1 %shard_map.286 = (bf16[512,1024]{1,0:T(8,128)(2,1)}, bf16[512,1024]{1,0:T(8,128)(2,1)}, bf16[512,1024]{1,0:T(8,128)(2,1)}) custom-call(bf16[512,1024]{1,0:T(8,128)(2,1)} %get-tuple-element.22.q_ref, bf16[512,1024]{1,0:T(8,128)(2,1)} %get-tuple-element.23.k_ref, bf16[512,1024]{1,0:T(8,128)(2,1)} %get-tuple-element.24.v_ref, bf16[512,1024]{1,0:T(8,128)(2,1)} %fusion.61.g_ref, ...), custom_call_target="tpu_custom_call" | custom-call | flops 2684354560 | bytes 7340032 | tf_op jit(solution)/shard_map/pallas_call | solution.py:157
  361.4 2.5 constant_dynamic-update-slice_fusion.2
  366.3 7.0 %multiply_reduce_fusion.1 = (f32[1024]{0:T(1024)S(1)}, f32[512]{0:T(512)S(1)}, f32[512,1024]{1,0:T(8,128)S(1)}) fusion(f32[512,1024]{1,0:T(8,128)S(1)} %copy-done.6, f32[512]{0:T(512)S(1)} %add_rsqrt_fusion.1, f32[1024]{0:T(1024)S(1)} %reshape.338, f32[1024]{0:T(1024)S(1)} %reshape.339, bf16[512,3072]{1,0:T(8,128)(2,1)} %constant_dynamic-update-slice_fusion, ...), kind=kOutput, calls=%fused_computation.67 | convolution fusion | flops 3224893952 | bytes 13647872 | tf_op jit(solution)/shard_map/dot_general | solution.py:24
  373.3 2.3 fusion.120
  376.5 27.1 %shard_map.287 = bf16[512,4096]{1,0:T(8,128)(2,1)} custom-call(s32[32]{0:T(128)} %get-tuple-element.75.order_ref, bf16[512,4096]{1,0:T(8,128)(2,1)} %get-tuple-element.117.in_ref), custom_call_target="tpu_custom_call" | custom-call | bytes 8388608 | tf_op jit(solution)/shard_map/pallas_call | solution.py:272
  403.6 2.6 fusion.122
  407.5 4.2 fusion.50
  413.9 9.2 %add_convert_fusion.8 = bf16[512,1024]{1,0:T(8,128)(2,1)} fusion(f32[512,1024]{1,0:T(8,128)S(1)} %get-tuple-element.116, bf16[512,4096]{1,0:T(8,128)(2,1)S(1)} %copy-done.4, bf16[4096,1024]{1,0:T(8,128)(2,1)} %all-gather.10.cloned.1.call-done, f32[1024]{0:T(1024)S(1)} %reshape.342), kind=kOutput, calls=%fused_computation.72 | convolution fusion | flops 4296540160 | bytes 15732736 | tf_op jit(solution)/shard_map/dot_general | solution.py:20
  423.1 3.6 fusion.129
  433.2 2.9 fusion.64
  436.1 3.2 collective-permute-done.4
  440.4 3.4 collective-permute-start.5
  443.7 5.0 fusion.27
  452.5 6.4 %fusion.17 = bf16[512,3072]{1,0:T(8,128)(2,1)S(1)} fusion(bf16[512,3072]{1,0:T(8,128)(2,1)} %collective-permute-done.9, bf16[512,3072]{1,0:T(8,128)(2,1)} %constant_dynamic-update-slice_fusion, bf16[512,512]{1,0:T(8,128)(2,1)S(1)} %collective-permute-done.8, bf16[512,512]{1,0:T(8,128)(2,1)S(1)} %copy-done.13), kind=kOutput, calls=%fused_computation.19 | convolution fusion | flops 3237478400 | bytes 10485760 | tf_op jit(solution)/shard_map/dot_general | solution.py:28
  459.7 4.8 collective-permute-start.7
  464.4 2.3 fusion.123
  469.1 8.3 %fusion.10 = bf16[512,4096]{1,0:T(8,128)(2,1)S(1)} fusion(bf16[512,4096]{1,0:T(8,128)(2,1)} %collective-permute-done.18, bf16[512,4096]{1,0:T(8,128)(2,1)} %get-tuple-element.79, bf16[512,512]{1,0:T(8,128)(2,1)} %copy-done.19, bf16[512,512]{1,0:T(8,128)(2,1)} %get-tuple-element.88), kind=kOutput, calls=%fused_computation.14 | convolution fusion | flops 4315938816 | bytes 13631488 | tf_op jit(solution)/shard_map/dot_general | solution.py:28
  480.3 4.0 collective-permute-start.27
  486.1 12.6 %collective-permute-done.12 = bf16[256,4096]{1,0:T(8,128)(2,1)S(1)} collective-permute-done((bf16[256,4096]{1,0:T(8,128)(2,1)S(1)}, bf16[256,4096]{1,0:T(8,128)(2,1)S(1)}, u32[]{:S(2)}, u32[]{:S(2)}) %collective-permute-start.12) | collective-permute-done | bytes 2097184 | tf_op jit(solution)/shard_map/ppermute | solution.py:210
  501.0 2.9 collective-permute-done.27
  505.4 27.0 %collective-permute-done.19 = bf16[256,4096]{1,0:T(8,128)(2,1)S(1)} collective-permute-done((bf16[256,4096]{1,0:T(8,128)(2,1)S(1)}, bf16[256,4096]{1,0:T(8,128)(2,1)S(1)}, u32[]{:S(2)}, u32[]{:S(2)}) %collective-permute-start.19) | collective-permute-done | bytes 2097184 | tf_op jit(solution)/shard_map/ppermute | solution.py:210
  533.3 4.5 collective-permute-start.20
  538.6 3.9 collective-permute-start.14
  542.6 30.0 %collective-permute-done.29 = bf16[256,1024]{1,0:T(8,128)(2,1)S(1)} collective-permute-done((bf16[256,1024]{1,0:T(8,128)(2,1)S(1)}, bf16[256,1024]{1,0:T(8,128)(2,1)S(1)}, u32[]{:S(2)}, u32[]{:S(2)}) %collective-permute-start.29) | collective-permute-done | bytes 524320 | tf_op jit(solution)/shard_map/ppermute | solution.py:210
  575.2 5.8 collective-permute-done.14
  583.0 21.4 %collective-permute-start.22 = (bf16[64,4096]{1,0:T(8,128)(2,1)S(1)}, bf16[64,4096]{1,0:T(8,128)(2,1)S(1)}, u32[]{:S(2)}, u32[]{:S(2)}) collective-permute-start(bf16[64,4096]{1,0:T(8,128)(2,1)S(1)} %slice.304), channel_id=1, source_target_pairs={{0,8},{1,9},{2,10},{3,11},{4,12},{5,13},{6,14},{7,15},{8,0},{9,1},... | collective-permute-start | bytes 1572872 | tf_op jit(solution)/shard_map/ppermute | solution.py:210
  604.6 5.3 collective-permute-start.16
  609.9 2.9 collective-permute-done.22
  613.5 2.1 collective-permute-done.16
  617.0 2.3 collective-permute-done.23
  (190 shorter events, 55.1 us)
Async XLA Ops:
  7.2 71.6 %all-gather.12.cloned.1.call-start = ((), (), s32[]{:S(2)}) async-start(), calls=%async_computation.3 | async-start | bytes 4866048 | tf_op jit(solution)/shard_map/all_gather | solution.py:323
  12.3 146.2 %all-gather.6.cloned.1.call-start = ((), (), s32[]{:S(2)}) async-start(), calls=%async_computation | async-start | bytes 8650752 | tf_op jit(solution)/shard_map/all_gather | solution.py:324
  14.0 223.3 %all-gather.8.cloned.1.call-start = ((), (), s32[]{:S(2)}) async-start(), calls=%async_computation.1 | async-start | bytes 8650752 | tf_op jit(solution)/shard_map/all_gather | solution.py:325
  14.8 301.4 %all-gather.10.cloned.1.call-start = ((), (), s32[]{:S(2)}) async-start(), calls=%async_computation.2 | async-start | bytes 8650752 | tf_op jit(solution)/shard_map/all_gather | solution.py:326
  22.9 3.5 copy-start
  24.4 382.6 %collective-permute-start = (bf16[512,1024]{1,0:T(8,128)(2,1)}, bf16[512,1024]{1,0:T(8,128)(2,1)}, u32[]{:S(2)}, u32[]{:S(2)}) collective-permute-start(bf16[512,1024]{1,0:T(8,128)(2,1)} %get-tuple-element.87), channel_id=1, source_target_pairs={{0,1},{1,0},{2,3},{3,2},{4,5},{5,4},{6,7},{7,6},{8,9},{9,8},{10,11... | collective-permute-start | bytes 3145736 | tf_op jit(solution)/shard_map/ppermute | solution.py:210
  91.7 66.9 %copy-start.5 = (f32[512,1024]{1,0:T(8,128)}, f32[512,1024]{1,0:T(8,128)S(1)}, u32[]{:S(2)}) copy-start(f32[512,1024]{1,0:T(8,128)S(1)} %get-tuple-element.114) | copy-start | bytes 6291460
  183.9 4.0 copy-start.18
  316.2 15.2 %copy-start.17 = (bf16[1024,4096]{1,0:T(8,128)(2,1)S(1)}, bf16[1024,4096]{1,0:T(8,128)(2,1)}, u32[]{:S(2)}) copy-start(bf16[1024,4096]{1,0:T(8,128)(2,1)} %all-gather.8.cloned.1.call-done) | copy-start | bytes 25165828
  339.8 89.6 %collective-permute-start.11 = (bf16[512,1024]{1,0:T(8,128)(2,1)}, bf16[512,1024]{1,0:T(8,128)(2,1)}, u32[]{:S(2)}, u32[]{:S(2)}) collective-permute-start(bf16[512,1024]{1,0:T(8,128)(2,1)} %fusion.119), channel_id=1, source_target_pairs={{0,1},{1,0},{2,3},{3,2},{4,5},{5,4},{6,7},{7,6},{8,9},{9,8},{10,11... | collective-permute-start | bytes 3145736 | tf_op jit(solution)/shard_map/ppermute | solution.py:210
  361.4 2.5 copy-start.10
  361.4 3.6 copy-start.9
  363.9 2.4 copy-start.6
  366.0 7.3 %copy-start.2 = (f32[512,1024]{1,0:T(8,128)S(1)}, f32[512,1024]{1,0:T(8,128)}, u32[]{:S(2)}) copy-start(f32[512,1024]{1,0:T(8,128)} %copy-done.1) | copy-start | bytes 6291460
  366.0 86.4 %collective-permute-start.9 = (bf16[512,3072]{1,0:T(8,128)(2,1)}, bf16[512,3072]{1,0:T(8,128)(2,1)}, u32[]{:S(2)}, u32[]{:S(2)}) collective-permute-start(bf16[512,3072]{1,0:T(8,128)(2,1)} %constant_dynamic-update-slice_fusion), channel_id=1, source_target_pairs={{0,1},{1,0},{2,3},{3,2},{4,5},{5,4},{6,7},{7,6},{8,9},{9,8},{10,11... | collective-permute-start | bytes 9437192 | tf_op jit(solution)/shard_map/ppermute | solution.py:210
  375.6 31.8 %collective-permute-start.1 = (bf16[512,1024]{1,0:T(8,128)(2,1)}, bf16[512,1024]{1,0:T(8,128)(2,1)}, u32[]{:S(2)}, u32[]{:S(2)}) collective-permute-start(bf16[512,1024]{1,0:T(8,128)(2,1)} %get-tuple-element.77), channel_id=1, source_target_pairs={{0,1},{1,0},{2,3},{3,2},{4,5},{5,4},{6,7},{7,6},{8,9},{9,8},{10,11... | collective-permute-start | bytes 3145736 | tf_op jit(solution)/shard_map/ppermute | solution.py:210
  376.2 30.2 %collective-permute-start.2 = (f32[32,256]{1,0:T(8,128)S(1)}, f32[32,256]{1,0:T(8,128)S(1)}, u32[]{:S(2)}, u32[]{:S(2)}) collective-permute-start(f32[32,256]{1,0:T(8,128)S(1)} %concatenate.76), channel_id=1, source_target_pairs={{0,1},{1,0},{2,3},{3,2},{4,5},{5,4},{6,7},{7,6},{8,9},{9,8},{10,11... | collective-permute-start | bytes 98312 | tf_op jit(solution)/shard_map/ppermute | solution.py:210
  403.6 2.6 copy-start.8
  406.3 22.5 %collective-permute-start.10 = (bf16[512,512]{1,0:T(8,128)(2,1)S(1)}, bf16[512,512]{1,0:T(8,128)(2,1)S(1)}, u32[]{:S(2)}, u32[]{:S(2)}) collective-permute-start(bf16[512,512]{1,0:T(8,128)(2,1)S(1)} %get-tuple-element.93), channel_id=1, source_target_pairs={{0,1},{1,0},{2,3},{3,2},{4,5},{5,4},{6,7},{7,6},{8,9},{9,8},{10,11... | collective-permute-start | bytes 1572872 | tf_op jit(solution)/shard_map/ppermute | solution.py:210
  407.0 33.3 %collective-permute-start.24 = (bf16[512,2048]{1,0:T(8,128)(2,1)S(1)}, bf16[512,2048]{1,0:T(8,128)(2,1)S(1)}, u32[]{:S(2)}, u32[]{:S(2)}) collective-permute-start(bf16[512,2048]{1,0:T(8,128)(2,1)S(1)} %get-tuple-element.81), channel_id=1, source_target_pairs={{0,1},{1,0},{2,3},{3,2},{4,5},{5,4},{6,7},{7,6},{8,9},{9,8},{10,11... | collective-permute-start | bytes 6291464 | tf_op jit(solution)/shard_map/ppermute | solution.py:210
  411.7 2.2 copy-start.4
  411.9 11.1 %copy-start.3 = (bf16[32,64,1024]{2,1,0:T(8,128)(2,1)S(1)}, bf16[32,64,1024]{2,1,0:T(8,128)(2,1)}, u32[]{:S(2)}) copy-start(bf16[32,64,1024]{2,1,0:T(8,128)(2,1)} %slice.257) | copy-start | bytes 12582916
  412.0 16.3 %collective-permute-start.3 = (bf16[576,1024]{1,0:T(8,128)(2,1)S(1)}, bf16[576,1024]{1,0:T(8,128)(2,1)S(1)}, u32[]{:S(2)}, u32[]{:S(2)}) collective-permute-start(bf16[576,1024]{1,0:T(8,128)(2,1)S(1)} %bitcast.68), channel_id=1, source_target_pairs={{0,4},{1,3},{2,6},{3,1},{4,0},{5,7},{6,2},{7,5},{8,12},{9,11},{10,... | collective-permute-start | bytes 3538952 | tf_op jit(solution)/shard_map/ppermute | solution.py:210
  428.2 40.1 %collective-permute-start.18 = (bf16[512,4096]{1,0:T(8,128)(2,1)}, bf16[512,4096]{1,0:T(8,128)(2,1)}, u32[]{:S(2)}, u32[]{:S(2)}) collective-permute-start(bf16[512,4096]{1,0:T(8,128)(2,1)} %get-tuple-element.79), channel_id=1, source_target_pairs={{0,1},{1,0},{2,3},{3,2},{4,5},{5,4},{6,7},{7,6},{8,9},{9,8},{10,11... | collective-permute-start | bytes 12582920 | tf_op jit(solution)/shard_map/ppermute | solution.py:210
  428.8 10.7 %collective-permute-start.25 = (bf16[512,1024]{1,0:T(8,128)(2,1)S(1)}, bf16[512,1024]{1,0:T(8,128)(2,1)S(1)}, u32[]{:S(2)}, u32[]{:S(2)}) collective-permute-start(bf16[512,1024]{1,0:T(8,128)(2,1)S(1)} %bitcast.58), channel_id=1, source_target_pairs={{0,1},{1,0},{2,3},{3,2},{4,5},{5,4},{6,7},{7,6},{8,9},{9,8},{10,11... | collective-permute-start | bytes 3145736 | tf_op jit(solution)/shard_map/ppermute | solution.py:210
  429.4 9.9 %collective-permute-start.4 = (bf16[288,1024]{1,0:T(8,128)(2,1)S(1)}, bf16[288,1024]{1,0:T(8,128)(2,1)S(1)}, u32[]{:S(2)}, u32[]{:S(2)}) collective-permute-start(bf16[288,1024]{1,0:T(8,128)(2,1)S(1)} %slice.273), channel_id=1, source_target_pairs={{0,2},{1,5},{2,0},{3,7},{4,6},{5,1},{6,4},{7,3},{8,10},{9,13},{10,... | collective-permute-start | bytes 1769480 | tf_op jit(solution)/shard_map/ppermute | solution.py:210
  433.2 6.1 copy-start.14
  439.3 12.5 %collective-permute-start.8 = (bf16[512,512]{1,0:T(8,128)(2,1)S(1)}, bf16[512,512]{1,0:T(8,128)(2,1)S(1)}, u32[]{:S(2)}, u32[]{:S(2)}) collective-permute-start(bf16[512,512]{1,0:T(8,128)(2,1)S(1)} %copy-done.14), channel_id=1, source_target_pairs={{0,1},{1,0},{2,3},{3,2},{4,5},{5,4},{6,7},{7,6},{8,9},{9,8},{10,11... | collective-permute-start | bytes 1572872 | tf_op jit(solution)/shard_map/ppermute | solution.py:210
  439.6 28.8 %collective-permute-start.17 = (bf16[512,512]{1,0:T(8,128)(2,1)}, bf16[512,512]{1,0:T(8,128)(2,1)S(1)}, u32[]{:S(2)}, u32[]{:S(2)}) collective-permute-start(bf16[512,512]{1,0:T(8,128)(2,1)} %get-tuple-element.89), channel_id=1, source_target_pairs={{0,1},{1,0},{2,3},{3,2},{4,5},{5,4},{6,7},{7,6},{8,9},{9,8},{10,11... | collective-permute-start | bytes 1572872 | tf_op jit(solution)/shard_map/ppermute | solution.py:210
  440.4 9.8 %collective-permute-start.5 = (bf16[144,1024]{1,0:T(8,128)(2,1)S(1)}, bf16[144,1024]{1,0:T(8,128)(2,1)S(1)}, u32[]{:S(2)}, u32[]{:S(2)}) collective-permute-start(bf16[144,1024]{1,0:T(8,128)(2,1)S(1)} %slice.275), channel_id=1, source_target_pairs={{0,8},{1,9},{2,10},{3,11},{4,12},{5,13},{6,14},{7,15},{24,16},{25,... | collective-permute-start | bytes 884744 | tf_op jit(solution)/shard_map/ppermute | solution.py:210
  448.7 3.7 copy-start.13
  450.2 29.0 %collective-permute-start.26 = (bf16[1024,1024]{1,0:T(8,128)(2,1)S(1)}, bf16[1024,1024]{1,0:T(8,128)(2,1)S(1)}, u32[]{:S(2)}, u32[]{:S(2)}) collective-permute-start(bf16[1024,1024]{1,0:T(8,128)(2,1)S(1)} %slice.311), channel_id=1, source_target_pairs={{0,4},{1,3},{2,6},{3,1},{4,0},{5,7},{6,2},{7,5},{8,12},{9,11},{10,... | collective-permute-start | bytes 6291464 | tf_op jit(solution)/shard_map/ppermute | solution.py:210
  451.8 7.8 %collective-permute-start.6 = (bf16[144,1024]{1,0:T(8,128)(2,1)S(1)}, bf16[144,1024]{1,0:T(8,128)(2,1)S(1)}, u32[]{:S(2)}, u32[]{:S(2)}) collective-permute-start(bf16[144,1024]{1,0:T(8,128)(2,1)S(1)} %add_convert_fusion.15), channel_id=1, source_target_pairs={{8,16},{9,17},{10,18},{11,19},{12,20},{13,21},{14,22},{15,23},{16,... | collective-permute-start | bytes 884744 | tf_op jit(solution)/shard_map/ppermute | solution.py:210
  459.0 39.7 %collective-permute-start.12 = (bf16[256,4096]{1,0:T(8,128)(2,1)S(1)}, bf16[256,4096]{1,0:T(8,128)(2,1)S(1)}, u32[]{:S(2)}, u32[]{:S(2)}) collective-permute-start(bf16[256,4096]{1,0:T(8,128)(2,1)S(1)} %pad_maximum_fusion), channel_id=1, source_target_pairs={{0,4},{1,3},{2,6},{3,1},{4,0},{5,7},{6,2},{7,5},{8,12},{9,11},{10,... | collective-permute-start | bytes 6291464 | tf_op jit(solution)/shard_map/ppermute | solution.py:210
  459.7 7.9 %collective-permute-start.7 = (bf16[72,1024]{1,0:T(8,128)(2,1)S(1)}, bf16[72,1024]{1,0:T(8,128)(2,1)S(1)}, u32[]{:S(2)}, u32[]{:S(2)}) collective-permute-start(bf16[72,1024]{1,0:T(8,128)(2,1)S(1)} %slice.277), channel_id=1, source_target_pairs={{0,8},{1,9},{2,10},{3,11},{4,12},{5,13},{6,14},{7,15},{8,0},{9,1},... | collective-permute-start | bytes 442376 | tf_op jit(solution)/shard_map/ppermute | solution.py:210
  477.6 54.8 %collective-permute-start.19 = (bf16[256,4096]{1,0:T(8,128)(2,1)S(1)}, bf16[256,4096]{1,0:T(8,128)(2,1)S(1)}, u32[]{:S(2)}, u32[]{:S(2)}) collective-permute-start(bf16[256,4096]{1,0:T(8,128)(2,1)S(1)} %slice.300), channel_id=1, source_target_pairs={{0,4},{1,3},{2,6},{3,1},{4,0},{5,7},{6,2},{7,5},{8,12},{9,11},{10,... | collective-permute-start | bytes 6291464 | tf_op jit(solution)/shard_map/ppermute | solution.py:210
  480.3 23.7 %collective-permute-start.27 = (bf16[512,1024]{1,0:T(8,128)(2,1)S(1)}, bf16[512,1024]{1,0:T(8,128)(2,1)S(1)}, u32[]{:S(2)}, u32[]{:S(2)}) collective-permute-start(bf16[512,1024]{1,0:T(8,128)(2,1)S(1)} %slice.313), channel_id=1, source_target_pairs={{0,8},{1,9},{2,10},{3,11},{4,12},{5,13},{6,14},{7,15},{24,16},{25,... | collective-permute-start | bytes 3145736 | tf_op jit(solution)/shard_map/ppermute | solution.py:210
  499.5 38.8 %collective-permute-start.13 = (bf16[128,4096]{1,0:T(8,128)(2,1)S(1)}, bf16[128,4096]{1,0:T(8,128)(2,1)S(1)}, u32[]{:S(2)}, u32[]{:S(2)}) collective-permute-start(bf16[128,4096]{1,0:T(8,128)(2,1)S(1)} %slice.289), channel_id=1, source_target_pairs={{0,2},{1,5},{2,0},{3,7},{4,6},{5,1},{6,4},{7,3},{8,10},{9,13},{10,... | collective-permute-start | bytes 3145736 | tf_op jit(solution)/shard_map/ppermute | solution.py:210
  504.4 33.4 %collective-permute-start.28 = (bf16[512,1024]{1,0:T(8,128)(2,1)S(1)}, bf16[512,1024]{1,0:T(8,128)(2,1)S(1)}, u32[]{:S(2)}, u32[]{:S(2)}) collective-permute-start(bf16[512,1024]{1,0:T(8,128)(2,1)S(1)} %add_convert_fusion.4), channel_id=1, source_target_pairs={{8,16},{9,17},{10,18},{11,19},{12,20},{13,21},{14,22},{15,23},{16,... | collective-permute-start | bytes 3145736 | tf_op jit(solution)/shard_map/ppermute | solution.py:210
  533.3 40.9 %collective-permute-start.20 = (bf16[128,4096]{1,0:T(8,128)(2,1)S(1)}, bf16[128,4096]{1,0:T(8,128)(2,1)S(1)}, u32[]{:S(2)}, u32[]{:S(2)}) collective-permute-start(bf16[128,4096]{1,0:T(8,128)(2,1)S(1)} %slice.302), channel_id=1, source_target_pairs={{0,8},{1,9},{2,10},{3,11},{4,12},{5,13},{6,14},{7,15},{24,16},{25,... | collective-permute-start | bytes 3145736 | tf_op jit(solution)/shard_map/ppermute | solution.py:210
  538.2 34.3 %collective-permute-start.29 = (bf16[256,1024]{1,0:T(8,128)(2,1)S(1)}, bf16[256,1024]{1,0:T(8,128)(2,1)S(1)}, u32[]{:S(2)}, u32[]{:S(2)}) collective-permute-start(bf16[256,1024]{1,0:T(8,128)(2,1)S(1)} %slice.315), channel_id=1, source_target_pairs={{0,8},{1,9},{2,10},{3,11},{4,12},{5,13},{6,14},{7,15},{8,0},{9,1},... | collective-permute-start | bytes 1572872 | tf_op jit(solution)/shard_map/ppermute | solution.py:210
  538.6 42.4 %collective-permute-start.14 = (bf16[64,4096]{1,0:T(8,128)(2,1)S(1)}, bf16[64,4096]{1,0:T(8,128)(2,1)S(1)}, u32[]{:S(2)}, u32[]{:S(2)}) collective-permute-start(bf16[64,4096]{1,0:T(8,128)(2,1)S(1)} %slice.291), channel_id=1, source_target_pairs={{0,8},{1,9},{2,10},{3,11},{4,12},{5,13},{6,14},{7,15},{24,16},{25,... | collective-permute-start | bytes 1572872 | tf_op jit(solution)/shard_map/ppermute | solution.py:210
  572.7 9.1 %collective-permute-start.30 = (bf16[128,1024]{1,0:T(8,128)(2,1)S(1)}, bf16[128,1024]{1,0:T(8,128)(2,1)S(1)}, u32[]{:S(2)}, u32[]{:S(2)}) collective-permute-start(bf16[128,1024]{1,0:T(8,128)(2,1)S(1)} %slice.317), channel_id=1, source_target_pairs={{0,2},{1,5},{2,0},{3,7},{4,6},{5,1},{6,4},{7,3},{8,10},{9,13},{10,... | collective-permute-start | bytes 786440 | tf_op jit(solution)/shard_map/ppermute | solution.py:210
  574.5 8.3 %collective-permute-start.21 = (bf16[128,4096]{1,0:T(8,128)(2,1)S(1)}, bf16[128,4096]{1,0:T(8,128)(2,1)S(1)}, u32[]{:S(2)}, u32[]{:S(2)}) collective-permute-start(bf16[128,4096]{1,0:T(8,128)(2,1)S(1)} %add_convert_fusion.6), channel_id=1, source_target_pairs={{8,16},{9,17},{10,18},{11,19},{12,20},{13,21},{14,22},{15,23},{16,... | collective-permute-start | bytes 3145736 | tf_op jit(solution)/shard_map/ppermute | solution.py:210
  581.2 23.2 %collective-permute-start.15 = (bf16[64,4096]{1,0:T(8,128)(2,1)S(1)}, bf16[64,4096]{1,0:T(8,128)(2,1)S(1)}, u32[]{:S(2)}, u32[]{:S(2)}) collective-permute-start(bf16[64,4096]{1,0:T(8,128)(2,1)S(1)} %add_convert_fusion.13), channel_id=1, source_target_pairs={{8,16},{9,17},{10,18},{11,19},{12,20},{13,21},{14,22},{15,23},{16,... | collective-permute-start | bytes 1572872 | tf_op jit(solution)/shard_map/ppermute | solution.py:210
  583.0 29.7 %collective-permute-start.22 = (bf16[64,4096]{1,0:T(8,128)(2,1)S(1)}, bf16[64,4096]{1,0:T(8,128)(2,1)S(1)}, u32[]{:S(2)}, u32[]{:S(2)}) collective-permute-start(bf16[64,4096]{1,0:T(8,128)(2,1)S(1)} %slice.304), channel_id=1, source_target_pairs={{0,8},{1,9},{2,10},{3,11},{4,12},{5,13},{6,14},{7,15},{8,0},{9,1},... | collective-permute-start | bytes 1572872 | tf_op jit(solution)/shard_map/ppermute | solution.py:210
  604.6 11.0 %collective-permute-start.16 = (bf16[32,4096]{1,0:T(8,128)(2,1)S(1)}, bf16[32,4096]{1,0:T(8,128)(2,1)S(1)}, u32[]{:S(2)}, u32[]{:S(2)}) collective-permute-start(bf16[32,4096]{1,0:T(8,128)(2,1)S(1)} %slice.293), channel_id=1, source_target_pairs={{0,8},{1,9},{2,10},{3,11},{4,12},{5,13},{6,14},{7,15},{8,0},{9,1},... | collective-permute-start | bytes 786440 | tf_op jit(solution)/shard_map/ppermute | solution.py:210
  612.9 6.4 %collective-permute-start.23 = (bf16[32,4096]{1,0:T(8,128)(2,1)S(1)}, bf16[32,4096]{1,0:T(8,128)(2,1)S(1)}, u32[]{:S(2)}, u32[]{:S(2)}) collective-permute-start(bf16[32,4096]{1,0:T(8,128)(2,1)S(1)} %slice.306), channel_id=1, source_target_pairs={{0,2},{1,5},{2,0},{3,7},{4,6},{5,1},{6,4},{7,3},{8,10},{9,13},{10,... | collective-permute-start | bytes 786440 | tf_op jit(solution)/shard_map/ppermute | solution.py:210
  (7 other events, 10.2 us)
Sparse Core Ops, SparseCore 0:
  12.4 66.3 all-gather.11
  82.2 76.2 all-gather.5
  161.4 75.9 all-gather.7
  240.1 76.0 all-gather.9

commit v2 on v1

v2 whole, which is shorter than its diff:
```python
import functools
import math

import jax
import jax.numpy as jnp
from jax import lax
from jax.experimental import pallas as pl
from jax.experimental.pallas import tpu as pltpu
from jax.sharding import PartitionSpec as P

HEADS = 16
HEAD = 64
EPSILON = 1e-06
AXES = ("dp", "fsdp")
F32 = jnp.float32
BF16 = jnp.bfloat16
VMEM = pltpu.CompilerParams(vmem_limit_bytes=48 << 20)


def dot(left, right, kind=F32):
    return jnp.dot(left, right, preferred_element_type=F32).astype(kind)


def against(left, right):
    return lax.dot_general(left, right, (((1,), (1,)), ((), ())), preferred_element_type=F32)


def contract(left, right):
    return lax.dot_general(left, right, (((0,), (0,)), ((), ())), preferred_element_type=F32)


def wide_tables(length):
    half = HEAD // 2
    indices = jnp.arange(half, dtype=F32)
    freqs = jnp.exp(indices * (-2.0 * math.log(10000.0) / HEAD))
    angles = jnp.arange(length, dtype=F32)[:, None] * freqs[None, :]
    cosine, sine = jnp.cos(angles), jnp.sin(angles)
    return (
        jnp.concatenate([cosine] * 4, axis=1),
        jnp.concatenate([-sine, sine, -sine, sine], axis=1),
    )


def swap_halves(values):
    half = HEAD // 2
    lane = lax.broadcasted_iota(jnp.int32, values.shape, 1)
    ahead = pltpu.roll(values, 2 * HEAD - half, 1)
    behind = pltpu.roll(values, half, 1)
    return jnp.where(lax.rem(lane, HEAD) < half, ahead, behind)


def allowed_of(column_ref, row_ref):
    length = row_ref.shape[-1]
    rows = lax.broadcasted_iota(jnp.int32, (length, length), 0)
    columns = lax.broadcasted_iota(jnp.int32, (length, length), 1)
    return (column_ref[0] == row_ref[0]) | (rows == columns)


def head_part(values, which):
    lane = lax.broadcasted_iota(jnp.int32, values.shape, 1)
    return jnp.where((lane >= HEAD) == (which == 1), values, jnp.zeros_like(values))


WIDE = 2 * HEAD
GROUP = 2


def attend_kernel(q_ref, k_ref, v_ref, cos_ref, sin_ref, column_ref, row_ref, qo_ref, ko_ref, vo_ref, a_ref, lse_ref):
    cosine, sine = cos_ref[...], sin_ref[...]
    allowed = allowed_of(column_ref, row_ref)
    for pair in range(GROUP):
        lanes = slice(pair * WIDE, (pair + 1) * WIDE)
        raw_q, raw_k = q_ref[:, lanes], k_ref[:, lanes]
        query = ((raw_q * cosine + swap_halves(raw_q) * sine)).astype(BF16)
        key = (raw_k * cosine + swap_halves(raw_k) * sine).astype(BF16)
        value = v_ref[:, lanes].astype(BF16)
        qo_ref[:, lanes] = query
        ko_ref[:, lanes] = key
        vo_ref[:, lanes] = value
        total = jnp.zeros(value.shape, F32)
        for which in range(2):
            scores = against(key, head_part(query, which)) * HEAD ** (-0.5)
            masked = jnp.where(allowed, scores, -1e30)
            highest = jnp.max(masked, axis=0, keepdims=True)
            exponent = jnp.exp(masked - highest)
            summed = jnp.sum(exponent, axis=0, keepdims=True)
            probs = (exponent / summed).astype(BF16)
            total += contract(probs, head_part(value, which))
            lse_ref[0, 0, pl.ds(2 * pair + which, 1), :] = highest + jnp.log(summed)
        a_ref[:, lanes] = total.astype(BF16)


def attend(mixed, tables, column, row, rows, length):
    width = HEADS * HEAD
    steps = HEADS // 2 // GROUP
    wide = WIDE * GROUP
    place = lambda shift: pl.BlockSpec((length, wide), lambda r, p, s=shift: (r, p + s))
    table = pl.BlockSpec((length, WIDE), lambda r, p: (0, 0))
    narrow = jax.ShapeDtypeStruct((rows * length, width), BF16)
    return pl.pallas_call(
        attend_kernel,
        grid=(rows, steps),
        in_specs=[
            place(0),
            place(steps),
            place(2 * steps),
            table,
            table,
            pl.BlockSpec((1, length, 1), lambda r, p: (r, 0, 0)),
            pl.BlockSpec((1, 1, length), lambda r, p: (r, 0, 0)),
        ],
        out_specs=[place(0)] * 4 + [pl.BlockSpec((1, 1, 2 * GROUP, length), lambda r, p: (r, p, 0, 0))],
        out_shape=[narrow] * 4 + [jax.ShapeDtypeStruct((rows, steps, 2 * GROUP, length), F32)],
        compiler_params=VMEM,
        cost_estimate=pl.CostEstimate(flops=rows * HEADS * length * length * 512, bytes_accessed=rows * length * width * 24, transcendentals=rows * HEADS * length * length),
    )(mixed, mixed, mixed, *tables, column, row)


def attend_back_kernel(q_ref, k_ref, v_ref, g_ref, lse_ref, cos_ref, sin_ref, column_ref, row_ref, gq_ref, gk_ref, gv_ref):
    cosine, sine = cos_ref[...], sin_ref[...]
    allowed = allowed_of(column_ref, row_ref)
    scale = HEAD ** (-0.5)
    for pair in range(GROUP):
        lanes = slice(pair * WIDE, (pair + 1) * WIDE)
        query, key, value, grad = q_ref[:, lanes], k_ref[:, lanes], v_ref[:, lanes], g_ref[:, lanes]
        grad_q = jnp.zeros(query.shape, F32)
        grad_k = jnp.zeros(query.shape, F32)
        grad_v = jnp.zeros(query.shape, F32)
        for which in range(2):
            own_query = head_part(query, which)
            own_grad = head_part(grad, which)
            mark = lse_ref[0, 0, pl.ds(2 * pair + which, 1), :]
            scores = against(key, own_query) * scale
            probs = jnp.exp(jnp.where(allowed, scores, -1e30) - mark)
            grad_probs = against(value, own_grad)
            inside = jnp.sum(grad_probs * probs, axis=0, keepdims=True)
            grad_scores = (probs * (grad_probs - inside)).astype(BF16)
            grad_v += dot(probs.astype(BF16), own_grad)
            grad_k += dot(grad_scores, own_query)
            grad_q += contract(grad_scores, head_part(key, which))
        grad_q = grad_q * scale
        grad_k = grad_k * scale
        gq_ref[:, lanes] = (grad_q * cosine - swap_halves(grad_q) * sine).astype(BF16)
        gk_ref[:, lanes] = (grad_k * cosine - swap_halves(grad_k) * sine).astype(BF16)
        gv_ref[:, lanes] = grad_v.astype(BF16)


def attend_back(query, key, value, grad, lse, tables, column, row, rows, length):
    width = HEADS * HEAD
    steps = HEADS // 2 // GROUP
    place = pl.BlockSpec((length, WIDE * GROUP), lambda r, p: (r, p))
    table = pl.BlockSpec((length, WIDE), lambda r, p: (0, 0))
    narrow = jax.ShapeDtypeStruct((rows * length, width), BF16)
    return pl.pallas_call(
        attend_back_kernel,
        grid=(rows, steps),
        in_specs=[place] * 4
        + [
            pl.BlockSpec((1, 1, 2 * GROUP, length), lambda r, p: (r, p, 0, 0)),
            table,
            table,
            pl.BlockSpec((1, length, 1), lambda r, p: (r, 0, 0)),
            pl.BlockSpec((1, 1, length), lambda r, p: (r, 0, 0)),
        ],
        out_specs=[place] * 3,
        out_shape=[narrow] * 3,
        compiler_params=VMEM,
        cost_estimate=pl.CostEstimate(flops=rows * HEADS * length * length * 1280, bytes_accessed=rows * length * width * 14, transcendentals=rows * HEADS * length * length),
    )(query, key, value, grad, lse, *tables, column, row)


def gelu_parts(values):
    cube = values * values
    arch = jnp.tanh(0.7978845608028654 * (values + 0.044715 * values * cube))
    slope = 0.5 * (1.0 + arch) + 0.5 * values * (1.0 - arch * arch) * (0.7978845608028654 * (1.0 + 3.0 * 0.044715 * cube))
    return 0.5 * values * (1.0 + arch), slope


TILE = 512
BLOCK = 128


def up_kernel(mine_ref, other_ref, core_ref, x_ref, w_ref, b_ref, act_ref, slope_ref, own_ref, give_ref):
    activated, slope = gelu_parts(dot(x_ref[...], w_ref[...]) + b_ref[...])
    activated = activated.astype(BF16)
    act_ref[...] = activated
    slope_ref[...] = slope.astype(BF16)
    second = core_ref[0] == 1
    pairs = TILE // 2 // BLOCK
    for pair in range(pairs):
        low = activated[:, 2 * pair * BLOCK : (2 * pair + 1) * BLOCK]
        high = activated[:, (2 * pair + 1) * BLOCK : (2 * pair + 2) * BLOCK]
        index = pl.program_id(0) * pairs + pair
        own_ref[:, pl.ds(pl.multiple_of(mine_ref[index] * BLOCK, BLOCK), BLOCK)] = jnp.where(second, high, low)
        give_ref[:, pl.ds(pl.multiple_of(other_ref[index] * BLOCK, BLOCK), BLOCK)] = jnp.where(second, low, high)


def up_product(normed, weight, bias, mine, other, core):
    tokens, width = normed.shape
    columns = weight.shape[1]
    tall = pl.BlockSpec((tokens, TILE), lambda i, *_: (0, i))
    whole = pl.BlockSpec((tokens, columns // 2), lambda i, *_: (0, 0))
    return pl.pallas_call(
        up_kernel,
        grid_spec=pltpu.PrefetchScalarGridSpec(
            num_scalar_prefetch=3,
            grid=(columns // TILE,),
            in_specs=[
                pl.BlockSpec((tokens, width), lambda i, *_: (0, 0)),
                pl.BlockSpec((width, TILE), lambda i, *_: (0, i)),
                pl.BlockSpec((1, TILE), lambda i, *_: (0, i)),
            ],
            out_specs=[tall, tall, whole, whole],
        ),
        out_shape=[jax.ShapeDtypeStruct((tokens, n), BF16) for n in (columns, columns, columns // 2, columns // 2)],
        compiler_params=VMEM,
        cost_estimate=pl.CostEstimate(flops=2 * tokens * width * columns, bytes_accessed=2 * (width * columns + 3 * tokens * columns), transcendentals=tokens * columns),
    )(mine, other, core, normed, weight, bias)


def inner_kernel(g_ref, w_ref, slope_ref, low_ref, sum_ref):
    grad_inner = against(g_ref[...], w_ref[...]) * slope_ref[...].astype(F32)
    low_ref[...] = grad_inner.astype(BF16)
    sum_ref[...] = jnp.sum(grad_inner, axis=0, keepdims=True)


def inner_back(grad_low, weight, slope):
    tokens, width = grad_low.shape
    columns = weight.shape[0]
    tall = pl.BlockSpec((tokens, TILE), lambda i: (0, i))
    return pl.pallas_call(
        inner_kernel,
        grid=(columns // TILE,),
        in_specs=[
            pl.BlockSpec((tokens, width), lambda i: (0, 0)),
            pl.BlockSpec((TILE, width), lambda i: (i, 0)),
            tall,
        ],
        out_specs=[tall, pl.BlockSpec((1, TILE), lambda i: (0, i))],
        out_shape=[jax.ShapeDtypeStruct((tokens, columns), BF16), jax.ShapeDtypeStruct((1, columns), F32)],
        compiler_params=VMEM,
        cost_estimate=pl.CostEstimate(flops=2 * tokens * width * columns, bytes_accessed=2 * (width * columns + 2 * tokens * columns), transcendentals=0),
    )(grad_low, weight, slope)


def pair_kernel(x_ref, xs_ref, g_ref, gs_ref, out_ref):
    out_ref[...] = (contract(x_ref[...], g_ref[...]) + contract(xs_ref[...], gs_ref[...])).astype(BF16)


def pair_product(x, x_other, g, g_other):
    tokens, rows = x.shape
    columns = g.shape[1]
    if rows > columns:
        steps = rows // TILE
        x_spec = pl.BlockSpec((tokens, TILE), lambda i: (0, i))
        g_spec = pl.BlockSpec((tokens, columns), lambda i: (0, 0))
        out_spec = pl.BlockSpec((TILE, columns), lambda i: (i, 0))
    else:
        tile = min(2 * TILE, columns // 2)
        steps = columns // tile
        x_spec = pl.BlockSpec((tokens, rows), lambda i: (0, 0))
        g_spec = pl.BlockSpec((tokens, tile), lambda i: (0, i))
        out_spec = pl.BlockSpec((rows, tile), lambda i: (0, i))
    return pl.pallas_call(
        pair_kernel,
        grid=(steps,),
        in_specs=[x_spec, x_spec, g_spec, g_spec],
        out_specs=out_spec,
        out_shape=jax.ShapeDtypeStruct((rows, columns), BF16),
        compiler_params=VMEM,
        cost_estimate=pl.CostEstimate(flops=4 * tokens * rows * columns, bytes_accessed=4 * tokens * (rows + columns) + 2 * rows * columns, transcendentals=0),
    )(x, x_other, g, g_other)


def norm_back(grad_normed, unit, scale, gain):
    scaled = grad_normed * gain
    return scale * (scaled - unit * jnp.mean(scaled * unit, axis=1, keepdims=True))


def pairs_of(move):
    pairs = []
    for z in range(4):
        for y in range(2):
            for x in range(2):
                for c in range(2):
                    there = move(z, y, x, c)
                    if there is not None:
                        source = ((z * 2 + y) * 2 + x) * 2 + c
                        target = ((there[0] * 2 + there[1]) * 2 + there[2]) * 2 + there[3]
                        pairs.append((source, target))
    return pairs


OTHER_CORE = pairs_of(lambda z, y, x, c: (z, y, x, 1 - c))
FIRST = pairs_of(lambda z, y, x, c: (z, 1 - y, x, c) if c == 0 else (z, y, 1 - x, c))
SECOND = pairs_of(lambda z, y, x, c: (z, y, 1 - x, c) if c == 0 else (z, 1 - y, x, c))
INWARD = pairs_of(lambda z, y, x, c: {0: (1, y, x, c), 3: (2, y, x, c)}.get(z))
MIDDLE = pairs_of(lambda z, y, x, c: {1: (2, y, x, c), 2: (1, y, x, c)}.get(z))
NEAR = pairs_of(lambda z, y, x, c: (z ^ 1, y, x, c))
Z_ORDER = ((3, 2, 1, 0), (3, 2, 0, 1), (0, 1, 3, 2), (0, 1, 2, 3))


def send(values, pairs):
    return lax.ppermute(values, AXES, pairs)


def block_order(place, late_plane, core):
    z, y, x = place
    levels = jnp.asarray(Z_ORDER, jnp.int32)[z]
    own_first = jnp.where(core == 0, y, x)
    own_second = jnp.where(core == 0, x, y)
    index = jnp.arange(16)
    if late_plane:
        first, slot, second = index // 8, index // 2 % 4, index % 2
    else:
        first, second, slot = index // 8, index // 4 % 2, index % 4
    level = jnp.sum(jnp.where(slot[:, None] == jnp.arange(4)[None, :], levels[None, :], 0), axis=1)
    first = jnp.where(first == 1, own_first, 1 - own_first)
    second = jnp.where(second == 1, own_second, 1 - own_second)
    at_y = jnp.where(core == 0, first, second)
    at_x = jnp.where(core == 0, second, first)
    return ((level * 2 + at_y) * 2 + at_x) * 2 + core


def both_orders(place, core, late_plane):
    return jnp.concatenate([block_order(place, late_plane, 1 - core), block_order(place, late_plane, core)])


def plus(left, right, kind=BF16):
    return (left.astype(F32) + right.astype(F32)).astype(kind)


OUTWARD = pairs_of(lambda z, y, x, c: {1: (0, y, x, c), 2: (3, y, x, c)}.get(z))


def collect(block, late_plane, inner):
    kept = block
    if late_plane:
        kept = jnp.concatenate([send(kept, SECOND), kept])
    near = jnp.concatenate([send(kept, NEAR), kept])
    far = send(near, MIDDLE)
    far = jnp.where(inner, far, send(far, OUTWARD))
    kept = jnp.concatenate([far, near])
    if not late_plane:
        kept = jnp.concatenate([send(kept, SECOND), kept])
    first = send(kept, FIRST)
    return first, kept, send(first, OTHER_CORE), send(kept, OTHER_CORE)


def place_kernel(order_ref, *refs):
    parts, out_ref, sems = refs[:4], refs[4], refs[5]
    block = out_ref.shape[0] // 32
    copies = []
    for index in range(32):
        part = parts[(2 + index // 8) % 4]
        target = out_ref.at[pl.ds(pl.multiple_of(order_ref[index] * block, block), block)]
        copies.append(pltpu.make_async_copy(part.at[pl.ds(index % 8 * block, block)], target, sems.at[index]))
        copies[-1].start()
    for copy in copies:
        copy.wait()


def placed(parts, order):
    rows, columns = parts[0].shape
    return pl.pallas_call(
        place_kernel,
        grid_spec=pltpu.PrefetchScalarGridSpec(
            num_scalar_prefetch=1,
            grid=(1,),
            in_specs=[pl.BlockSpec((rows, columns), lambda i, order: (0, 0))] * 4,
            out_specs=pl.BlockSpec(memory_space=pl.ANY),
            scratch_shapes=[pltpu.SemaphoreType.DMA((32,))],
        ),
        out_shape=jax.ShapeDtypeStruct((4 * rows, columns), parts[0].dtype),
        compiler_params=VMEM,
        cost_estimate=pl.CostEstimate(flops=0, bytes_accessed=16 * rows * columns, transcendentals=0),
    )(order, *parts)


def after(value, *others):
    return lax.optimization_barrier((value,) + others)[0]


class Summing:
    def __init__(self, values, late_plane):
        self.kept = values
        self.far = None
        self.steps = [FIRST, INWARD, MIDDLE, NEAR, SECOND] if late_plane else [FIRST, SECOND, INWARD, MIDDLE, NEAR]

    def step(self):
        pairs = self.steps.pop(0)
        kept, half = self.kept, self.kept.shape[0] // 2
        if pairs is INWARD:
            self.far = plus(kept[:half], send(kept[:half], pairs))
            self.kept = kept[half:]
        elif pairs is MIDDLE:
            self.kept = plus(kept, send(self.far, pairs))
            self.far = None
        else:
            self.kept = plus(kept[half:], send(kept[:half], pairs), BF16 if self.steps else F32)
        return self.kept if self.far is None else self.far

    def finish(self):
        while self.steps:
            self.step()
        return self.kept


def picked(values, order):
    columns = values.shape[1]
    block = columns // 32
    column = jnp.arange(columns)
    source = jnp.repeat(order, block) * block + column % block
    choice = (column[:, None] == source[None, :]).astype(BF16)
    return dot(values, choice, BF16)


def swapped(values):
    return send(values, OTHER_CORE)


def halves(values):
    half = values.shape[1] // 2
    return values[:, :half], values[:, half:]


def on_device(
    known,
    frames,
    skip,
    cotangent,
    segment_ids,
    row_lengths,
    w_skip,
    b_skip,
    gain_one,
    w_qkv,
    w_out,
    gain_two,
    w_up,
    b_up,
    w_down,
    b_down,
):
    micro, rows, length, width = frames.shape
    count = micro * rows
    tokens = count * length
    devices = width // gain_one.shape[0]
    hidden_width = w_up.shape[1]

    vectors = jnp.concatenate([b_skip, gain_one, gain_two, b_down, b_up])
    part = w_skip.shape[0]
    lines = -(-vectors.shape[0] // width)
    lines = -(-lines // 8) * 8
    padded = jnp.pad(vectors, (0, lines * width - vectors.shape[0])).reshape(lines, width)
    own_skip = jnp.concatenate([w_skip, padded])
    own_qkv = jnp.concatenate([w_qkv, w_out], axis=1)
    if known:
        place = lax.axis_index("dp")
        at_x = lax.axis_index("fsdp")
        core = at_x % 2
        coords = (place // 2, place % 2, at_x // 2)
        late = both_orders(coords, core, True)
        early = both_orders(coords, core, False)
        inner_chip = (coords[0] == 1) | (coords[0] == 2)
        all_up = lax.all_gather(w_up, AXES, axis=0, tiled=True)
        all_down = lax.all_gather(w_down, AXES, axis=0, tiled=True)
        all_skip = placed(collect(own_skip, True, inner_chip), late).reshape(devices, part + lines, width)
        all_qkv = placed(collect(own_qkv, False, inner_chip), early)
    else:
        all_skip = lax.all_gather(own_skip, AXES, axis=0, tiled=False)
        all_qkv = lax.all_gather(own_qkv, AXES, axis=0, tiled=True)
        all_up = lax.all_gather(w_up, AXES, axis=0, tiled=True)
        all_down = lax.all_gather(w_down, AXES, axis=0, tiled=True)
    full_skip = all_skip[:, :part].reshape(devices * part, width)
    flat = all_skip[:, part:].reshape(devices, lines * width)
    small = width // devices
    spread = lambda at, size: flat[:, at : at + size].reshape(1, devices * size).astype(F32)
    bias_skip, gain_1, gain_2, bias_down = (spread(i * small, small) for i in range(4))
    bias_up = spread(4 * small, hidden_width // devices)
    full_qkv = all_qkv[:, : 3 * width]
    full_out = all_qkv[:, 3 * width :]

    frames = frames.reshape(tokens, width)
    skip = skip.reshape(tokens, width)
    grad_low = cotangent.reshape(tokens, width)
    grad_out = grad_low.astype(F32)
    segments = segment_ids.reshape(count, length)
    lengths = row_lengths.reshape(count, 1)
    reach = jnp.where(jnp.arange(length)[None, :] < lengths, segments, -1)
    column, row = reach[:, :, None], segments[:, None, :]
    tables = wide_tables(length)

    joined = jnp.concatenate([frames, skip], axis=1)
    hidden = dot(joined, full_skip) + bias_skip
    scale_one = lax.rsqrt(jnp.mean(hidden * hidden, axis=1, keepdims=True) + EPSILON)
    unit_one = hidden * scale_one
    normed_one = (unit_one * gain_1).astype(BF16)
    mixed = dot(normed_one, full_qkv)
    query, key, value, attended, lse = attend(mixed, tables, column, row, count, length)
    middle = hidden + dot(attended, full_out)
    scale_two = lax.rsqrt(jnp.mean(middle * middle, axis=1, keepdims=True) + EPSILON)
    unit_two = middle * scale_two
    normed_two = (unit_two * gain_2).astype(BF16)
    total = lambda values: jnp.sum(values, axis=0)
    back = functools.partial(attend_back, query, key, value, lse=lse, tables=tables, column=column, row=row, rows=count, length=length)

    if known:
        ends = lambda order: jnp.sum(jnp.where(order[None, :] // 2 == jnp.arange(16)[:, None], jnp.arange(16)[None, :], 0), axis=1).astype(jnp.int32)
        give_joined, own_joined = halves(picked(joined, early))
        joined_other = swapped(give_joined)
        grad_other = swapped(grad_low)
        give_one, own_one = halves(picked(normed_one, early))
        give_attended, own_attended = halves(picked(attended, early))
        give_two, own_two = halves(picked(normed_two, late))
        one_other, attended_other, two_other = swapped(give_one), swapped(give_attended), swapped(give_two)

        activated, slope, own_active, give_active = up_product(
            normed_two, all_up, bias_up, ends(late[16:]), ends(late[:16]), core.reshape(1)
        )
        active_other = swapped(give_active)
        inner_low, inner_sum = inner_back(grad_low, all_down, slope)
        inner_other = swapped(inner_low)
        g_down = pair_product(own_active, active_other, grad_low, grad_other)
        down = Summing(g_down, True)
        inner_low = after(inner_low, g_down)
        grad_normed_two = against(inner_low, all_up)
        g_up = pair_product(own_two, two_other, after(inner_low, grad_normed_two), inner_other)
        up = Summing(g_up, True)
        grad_middle = grad_out + norm_back(after(grad_normed_two, g_up), unit_two, scale_two, gain_2)
        middle_low = grad_middle.astype(BF16)
        middle_other = swapped(middle_low)
        grad_attended = against(middle_low, full_out).astype(BF16)
        grad_mixed = jnp.concatenate(back(grad=after(grad_attended, down.step())), axis=1)
        mixed_other = swapped(grad_mixed)
        g_out = pair_product(own_attended, attended_other, after(middle_low, up.step(), down.step()), middle_other)
        grad_normed_one = against(grad_mixed, full_qkv)
        g_qkv = pair_product(own_one, one_other, after(grad_mixed, g_out), mixed_other)
        both = Summing(jnp.concatenate([g_qkv, g_out], axis=1), False)
        grad_normed_one = after(grad_normed_one, up.step(), down.step())
        grad_hidden = grad_middle + norm_back(grad_normed_one, unit_one, scale_one, gain_1)
        hidden_low = grad_hidden.astype(BF16)
        g_skip = pair_product(own_joined, joined_other, hidden_low, swapped(hidden_low))
        vector_grads = (total(grad_hidden), total(grad_normed_one * unit_one), total(grad_normed_two * unit_two), total(grad_out), inner_sum[0])
        by_block = jnp.concatenate([v.reshape(devices, -1) for v in vector_grads], axis=1)
        by_block = by_block + swapped(by_block)
        choice = (early[16:, None] == jnp.arange(devices)[None, :]).astype(F32)
        by_block = jnp.dot(choice, by_block, precision=lax.Precision.HIGHEST).astype(BF16)
        by_block = jnp.pad(by_block, ((0, 0), (0, lines * width - by_block.shape[1])))
        g_last = jnp.concatenate([g_skip.reshape(16, part, width), by_block.reshape(16, lines, width)], axis=1)
        tail = Summing(g_last.reshape(16 * (part + lines), width), False)
        grad_joined = against(after(hidden_low, g_last, both.step(), up.step(), down.step()), full_skip)
        output = (middle + (dot(after(activated, grad_joined, tail.step(), both.step()), all_down) + bias_down)).astype(BF16)
        down_grad = down.finish()
        up_grad = up.finish()
        both_grad = both.finish()
        last = tail.finish()
        qkv_grad, out_grad = both_grad[:, : 3 * width], both_grad[:, 3 * width :]
        skip_weight_grad = last[:part]
        line = last[part:].reshape(lines * width)
        shares = [line[i * small : (i + 1) * small] for i in range(4)]
        shares.append(line[4 * small : 4 * small + hidden_width // devices])
        grad_joined = against(after(hidden_low, g_last), full_skip)
        output = (middle + (dot(after(activated, g_last), all_down) + bias_down)).astype(BF16)
    else:
        activated, slope = gelu_parts(dot(normed_two, all_up) + bias_up)
        activated = activated.astype(BF16)
        output = (middle + (dot(activated, all_down) + bias_down)).astype(BF16)
        grad_inner = against(grad_low, all_down) * slope
        inner_low = grad_inner.astype(BF16)
        grad_normed_two = against(inner_low, all_up)
        grad_middle = grad_out + norm_back(grad_normed_two, unit_two, scale_two, gain_2)
        middle_low = grad_middle.astype(BF16)
        grad_mixed = jnp.concatenate(back(grad=against(middle_low, full_out).astype(BF16)), axis=1)
        grad_normed_one = against(grad_mixed, full_qkv)
        grad_hidden = grad_middle + norm_back(grad_normed_one, unit_one, scale_one, gain_1)
        hidden_low = grad_hidden.astype(BF16)
        grad_joined = against(hidden_low, full_skip)
        vector_grads = (total(grad_hidden), total(grad_normed_one * unit_one), total(grad_normed_two * unit_two), total(grad_out), total(grad_inner))
        scatter = lambda values: lax.psum_scatter(values, AXES, scatter_dimension=0, tiled=True)
        down_grad = scatter(contract(activated, grad_low))
        up_grad = scatter(contract(normed_two, inner_low))
        out_grad = scatter(contract(attended, middle_low))
        qkv_grad = scatter(contract(normed_one, grad_mixed))
        skip_weight_grad = scatter(contract(joined, hidden_low))
        shares = [scatter(v) for v in vector_grads]

    shape = (micro, rows, length, width)
    return (
        output.reshape(shape),
        grad_joined[:, :width].reshape(shape),
        grad_joined[:, width:].reshape(shape),
        skip_weight_grad,
        shares[0],
        shares[1],
        qkv_grad,
        out_grad,
        shares[2],
        up_grad,
        shares[4],
        down_grad,
        shares[3],
    )


def solution(mesh):
    known = mesh.shape["dp"] == 8 and mesh.shape["fsdp"] == 4
    tokens = P(None, AXES, None, None)
    weight = P(AXES, None)
    vector = P(AXES)
    return jax.shard_map(
        functools.partial(on_device, known),
        mesh=mesh,
        in_specs=(
            tokens,
            tokens,
            tokens,
            P(None, AXES, None),
            P(None, AXES),
            weight,
            vector,
            vector,
            weight,
            weight,
            vector,
            weight,
            vector,
            weight,
            vector,
        ),
        out_specs=(
            tokens,
            tokens,
            tokens,
            weight,
            vector,
            vector,
            weight,
            weight,
            vector,
            weight,
            vector,
            weight,
            vector,
        ),
        check_vma=False,
    )
```

time: 637 us -> 525 us (0.82)
  waiting for transfers between devices: 320 us -> 145 us
  matrix products: 115 us -> 63.1 us
  starting transfers between devices: 64.1 us -> 115 us
  Pallas kernels: 61.4 us -> 90.7 us
  other arithmetic: 19.7 us -> 38.9 us
  local copies, waits for them, and re-layouts: 32.1 us -> 50.9 us
    all_gather x2 -> x0, waiting for transfers between devices: 113 us -> none  [the longest x1 63.6 us: on_device(): lax.all_gather(jnp.concatenate([w_qkv, w_out], axis=1), AXES, axis=0, til...]
    all_gather x1, waiting for transfers between devices: 65.9 us -> 0.01 us  [on_device(): all_down = lax.all_gather(w_down, AXES, axis=0, tiled=True)]
    ppermute x31 -> x45, starting transfers between devices: 63.9 us -> 115 us  [send(): return lax.ppermute(values, AXES, pairs)]
    ppermute x31 -> x45, waiting for transfers between devices: 92.4 us -> 143 us  [send(): return lax.ppermute(values, AXES, pairs)]
    all_gather x1, waiting for transfers between devices: 47.1 us -> 0.02 us  [on_device(): all_up = lax.all_gather(w_up, AXES, axis=0, tiled=True)]
    pallas_call x3 -> x11, Pallas kernels: 61.4 us -> 90.7 us  [the longest x5 29.2 us: pair_product(): pl.pallas_call(pair_kernel, grid=(steps,), in_specs=[x_spec, x_spec, g_sp...]
    dot_general x5 -> x0, matrix products: 26.8 us -> none  [contract(): lax.dot_general(left, right, (((0,), (0,)), ((), ())), preferred_element_...]
    dot_general x5 -> x4, matrix products: 36.8 us -> 21.4 us  [against(): lax.dot_general(left, right, (((1,), (1,)), ((), ())), preferred_element_...]
  transfers between devices with their start and end apart: 35 -> 47, of which waited for: 16 -> 16; matrix products, arithmetic and copies ran while one was open for 25% -> 27% of each run, Pallas kernels for 10% -> 17%
where the time goes in v2:
time: 525 us; the launch traced here: 519 us
  waiting for transfers between devices  145 us (28%)
  starting transfers between devices  115 us (22%)
  Pallas kernels  90.7 us (17%)
  matrix products  63.1 us (12%)
  local copies, waits for them, and re-layouts  50.9 us (10%)
  other arithmetic  38.9 us (7%)
  between operations  15.8 us (3%)
    ppermute x45, waiting for transfers between devices, send(): return lax.ppermute(values, AXES, pairs)  143 us
    ppermute x45, starting transfers between devices, send(): return lax.ppermute(values, AXES, pairs)  115 us
    dot_general x8, matrix products, dot(): return jnp.dot(left, right, preferred_element_type=F32).astype(kind)  41.5 us
    pallas_call x5, Pallas kernels, pair_product(): pl.pallas_call(pair_kernel, grid=(steps,), in_specs=[x_spec, x_spec, g_sp...  29.2 us
    dot_general x4, matrix products, against(): lax.dot_general(left, right, (((1,), (1,)), ((), ())), preferred_element_...  21.4 us
    unnamed x178, local copies, waits for them, and re-layouts  17.6 us
    pallas_call x1, Pallas kernels, up_product(): pl.pallas_call(up_kernel, grid_spec=pltpu.PrefetchScalarGridSpec(num_scal...  15.5 us
    convert_element_type x16, other arithmetic, plus(): return (left.astype(F32) + right.astype(F32)).astype(kind)  13.4 us
  transfers between devices with their start and end apart: 47, of which 16 were waited for; matrix products, arithmetic and copies ran while one was open for 27% of the time, Pallas kernels for 17%

profile of v2, /device:TPU:0, one launch (start us, length us, event | category | flops | bytes accessed | tf_op | source)
XLA Modules:
  0.0 519.3 jit_solution(7053052061158094902)
XLA Ops:
  10.5 3.0 collective-permute-start.7
  13.5 6.3 %collective-permute-done.7 = bf16[32,4096]{1,0:T(8,128)(2,1)S(1)} collective-permute-done((bf16[32,4096]{1,0:T(8,128)(2,1)S(1)}, bf16[32,4096]{1,0:T(8,128)(2,1)S(1)}, u32[]{:S(2)}, u32[]{:S(2)}) %collective-permute-start.7) | collective-permute-done | bytes 262176 | tf_op jit(solution)/shard_map/ppermute | solution.py:304
  23.8 4.6 collective-permute-done
  28.4 23.5 %collective-permute-start.1 = (bf16[144,1024]{1,0:T(8,128)(2,1)S(1)}, bf16[144,1024]{1,0:T(8,128)(2,1)S(1)}, u32[]{:S(2)}, u32[]{:S(2)}) collective-permute-start(bf16[144,1024]{1,0:T(8,128)(2,1)S(1)} %pad_maximum_fusion.9), channel_id=1, source_target_pairs={{0,8},{1,9},{2,10},{3,11},{4,12},{5,13},{6,14},{7,15},{8,0},{9,1},... | collective-permute-start | bytes 884744 | tf_op jit(solution)/shard_map/ppermute | solution.py:304
  51.9 13.8 %collective-permute-done.9 = bf16[64,4096]{1,0:T(8,128)(2,1)S(1)} collective-permute-done((bf16[64,4096]{1,0:T(8,128)(2,1)S(1)}, bf16[64,4096]{1,0:T(8,128)(2,1)S(1)}, u32[]{:S(2)}, u32[]{:S(2)}) %collective-permute-start.9) | collective-permute-done | bytes 524320 | tf_op jit(solution)/shard_map/ppermute | solution.py:304
  67.4 13.7 %collective-permute-done.1 = bf16[144,1024]{1,0:T(8,128)(2,1)S(1)} collective-permute-done((bf16[144,1024]{1,0:T(8,128)(2,1)S(1)}, bf16[144,1024]{1,0:T(8,128)(2,1)S(1)}, u32[]{:S(2)}, u32[]{:S(2)}) %collective-permute-start.1) | collective-permute-done | bytes 294944 | tf_op jit(solution)/shard_map/ppermute | solution.py:304
  87.5 6.8 %collective-permute-done.10 = bf16[128,4096]{1,0:T(8,128)(2,1)} collective-permute-done((bf16[128,4096]{1,0:T(8,128)(2,1)S(1)}, bf16[128,4096]{1,0:T(8,128)(2,1)}, u32[]{:S(2)}, u32[]{:S(2)}) %collective-permute-start.10) | collective-permute-done | bytes 1048608 | tf_op jit(solution)/shard_map/ppermute | solution.py:304
  97.5 26.0 %collective-permute-done.3 = bf16[288,1024]{1,0:T(8,128)(2,1)S(1)} collective-permute-done((bf16[288,1024]{1,0:T(8,128)(2,1)}, bf16[288,1024]{1,0:T(8,128)(2,1)S(1)}, u32[]{:S(2)}, u32[]{:S(2)}) %collective-permute-start.3) | collective-permute-done | bytes 589856 | tf_op jit(solution)/shard_map/ppermute | solution.py:304
  132.2 15.4 %collective-permute-done.4.refs_0_ = bf16[576,1024]{1,0:T(8,128)(2,1)} collective-permute-done((bf16[576,1024]{1,0:T(8,128)(2,1)}, bf16[576,1024]{1,0:T(8,128)(2,1)}, u32[]{:S(2)}, u32[]{:S(2)}) %collective-permute-start.4) | collective-permute-done | bytes 1179680 | tf_op jit(solution)/shard_map/ppermute | solution.py:304
  150.3 7.8 %fusion.9 = bf16[512,2048]{1,0:T(8,128)(2,1)} fusion(s32[2048]{0:T(1024)S(1)} %fusion.34, bf16[512,1024]{1,0:T(8,128)(2,1)} %bitcast.75, bf16[512,1024]{1,0:T(8,128)(2,1)} %bitcast.77), kind=kOutput, calls=%fused_computation.20 | convolution fusion | flops 4304404480 | bytes 4202496 | tf_op jit(solution)/shard_map/dot_general | solution.py:21
  158.2 4.8 shard_map.282
  164.1 4.9 slice.249
  174.3 5.3 %multiply_reduce_fusion.5 = (f32[512]{0:T(512)S(1)}, f32[512,1024]{1,0:T(8,128)S(1)}) fusion(f32[1024]{0:T(1024)} %reshape.475, bf16[2048,1024]{1,0:T(8,128)(2,1)} %bitcast.61, bf16[512,1024]{1,0:T(8,128)(2,1)} %bitcast.76, bf16[512,1024]{1,0:T(8,128)(2,1)} %bitcast.78), kind=kOutput, calls=%fused_computation.46 | convolution fusion | flops 2153250304 | bytes 8394752 | tf_op jit(solution)/shard_map/dot_general | solution.py:21
  180.4 6.9 %shard_map.283 = bf16[1024,4096]{1,0:T(8,128)(2,1)} custom-call(s32[32]{0:T(128)S(1)} %copy-done.12, bf16[256,4096]{1,0:T(8,128)(2,1)} %collective-permute-done.11.refs_0_, bf16[256,4096]{1,0:T(8,128)(2,1)S(1)} %pad_maximum_fusion.3.refs_1_, bf16[256,4096]{1,0:T(8,128)(2,1)} %collective-permute-done.12.refs_2_, bf16[256,4096]{1,0:T(8,128)(2,1)} %collective-permute-done.13.refs_3_), custom_call_target="tpu_custom_call" | custom-call | bytes 16777216 | tf_op jit(solution)/shard_map/pallas_call | solution.py:365
  187.4 8.6 %fusion.4.q_ref.k_ref.v_ref = f32[512,3072]{1,0:T(8,128)} fusion(bf16[1024,4096]{1,0:T(8,128)(2,1)} %shard_map.283, f32[512,1024]{1,0:T(8,128)S(1)} %get-tuple-element.142, f32[1024]{0:T(1024)S(1)} %copy-done.62, f32[512]{0:T(512)S(1)} %add_rsqrt_fusion.1, f32[1024]{0:T(1024)S(1)} %copy-done.60), kind=kOutput, calls=%fused_computation.5 | convolution fusion | flops 3223322624 | bytes 14690304 | tf_op jit(solution)/shard_map/dot_general | solution.py:21
  196.0 11.5 %shard_map.284 = (bf16[512,1024]{1,0:T(8,128)(2,1)S(1)}, bf16[512,1024]{1,0:T(8,128)(2,1)S(1)}, bf16[512,1024]{1,0:T(8,128)(2,1)S(1)}, bf16[512,1024]{1,0:T(8,128)(2,1)S(1)}, f32[2,4,4,256]{3,2,1,0:T(4,128)S(1)}) custom-call(f32[512,3072]{1,0:T(8,128)} %fusion.4.q_ref.k_ref.v_ref, f32[512,3072]{1,0:T(8,128)} %fusion.4.q_ref.k_ref.v_ref, ...), custom_call_target="tpu_custom_call" | custom-call | flops 1073741824 | bytes 12582912 | tf_op jit(solution)/shard_map/pallas_call | solution.py:100
  207.5 4.1 multiply_reduce_fusion.4
  214.6 15.5 %shard_map.285 = (bf16[512,4096]{1,0:T(8,128)(2,1)}, bf16[512,4096]{1,0:T(8,128)(2,1)}, bf16[512,2048]{1,0:T(8,128)(2,1)S(1)}, bf16[512,2048]{1,0:T(8,128)(2,1)}) custom-call(s32[16]{0:T(128)S(1)} %copy-done.20, s32[16]{0:T(128)S(1)} %copy-done.21, s32[1]{0:T(128)} %bitcast.6.core_ref, bf16[512,1024]{1,0:T(8,128)(2,1)S(1)} %multiply_convert_fusion.x_ref, ...), custom_call_target="tpu_custom_call" | custom-call | flops 4294967296 | bytes 20971520 | tf_op jit(solution)/shard_map/pallas_call | solution.py:203
  233.9 11.2 %shard_map.286 = (bf16[512,4096]{1,0:T(8,128)(2,1)}, f32[1,4096]{1,0:T(1,128)S(1)}) custom-call(bf16[512,1024]{1,0:T(8,128)(2,1)S(1)} %bitcast.53, bf16[4096,1024]{1,0:T(8,128)(2,1)} %all-gather.5.cloned.1.call-done.w_ref, bf16[512,4096]{1,0:T(8,128)(2,1)} %get-tuple-element.38.slope_ref), custom_call_target="tpu_custom_call" | custom-call | flops 4294967296 | bytes 16777216 | tf_op jit(solution)/shard_map/pallas_call | solution.py:231
  248.8 3.0 fusion.25
  255.8 7.8 %shard_map.287 = bf16[2048,1024]{1,0:T(8,128)(2,1)} custom-call(bf16[512,2048]{1,0:T(8,128)(2,1)S(1)} %copy-done.23, bf16[512,2048]{1,0:T(8,128)(2,1)} %collective-permute-done.15.xs_ref, bf16[512,1024]{1,0:T(8,128)(2,1)S(1)} %bitcast.54, bf16[512,1024]{1,0:T(8,128)(2,1)} %collective-permute-done.16.gs_ref), custom_call_target="tpu_custom_call" | custom-call | flops 4294967296 | bytes 10485760 | tf_op jit(solution)/shard_map/pallas_call | solution.py:264
  269.4 8.4 %fusion.69 = f32[512,1024]{1,0:T(8,128)S(1)} fusion(bf16[512,4096]{1,0:T(8,128)(2,1)} %get-tuple-element.43.g_ref, bf16[1024,4096]{1,0:T(8,128)(2,1)} %all-gather.3.cloned.1.call-done.w_ref), kind=kOutput, calls=%fused_computation.208 | convolution fusion | flops 4294967296 | bytes 14680064 | tf_op jit(solution)/shard_map/dot_general | solution.py:25
  277.8 13.6 %collective-permute-done.19 = bf16[1024,1024]{1,0:T(8,128)(2,1)S(1)} collective-permute-done((bf16[1024,1024]{1,0:T(8,128)(2,1)S(1)}, bf16[1024,1024]{1,0:T(8,128)(2,1)S(1)}, u32[]{:S(2)}, u32[]{:S(2)}) %collective-permute-start.19) | collective-permute-done | bytes 2097184 | tf_op jit(solution)/shard_map/ppermute | solution.py:304
  293.6 11.4 %collective-permute-start.22 = (bf16[512,1024]{1,0:T(8,128)(2,1)}, bf16[512,1024]{1,0:T(8,128)(2,1)S(1)}, u32[]{:S(2)}, u32[]{:S(2)}) collective-permute-start(bf16[512,1024]{1,0:T(8,128)(2,1)} %slice.267), channel_id=1, source_target_pairs={{0,8},{1,9},{2,10},{3,11},{4,12},{5,13},{6,14},{7,15},{24,16},{25,... | collective-permute-start | bytes 3145736 | tf_op jit(solution)/shard_map/ppermute | solution.py:304
  305.1 7.4 %shard_map.288 = bf16[512,4096]{1,0:T(8,128)(2,1)S(1)} custom-call(bf16[512,512]{1,0:T(8,128)(2,1)S(1)} %get-tuple-element.125.x_ref, bf16[512,512]{1,0:T(8,128)(2,1)S(1)} %collective-permute-done.17.xs_ref, bf16[512,4096]{1,0:T(8,128)(2,1)} %get-tuple-element.43.g_ref, bf16[512,4096]{1,0:T(8,128)(2,1)} %collective-permute-done.18.gs_ref), custom_call_target="tpu_custom_call" | custom-call | flops 4294967296 | bytes 13631488 | tf_op jit(solution)/shard_map/pallas_call | solution.py:264
  317.3 4.0 fusion.21.g_ref
  321.4 11.6 %shard_map.289 = (bf16[512,1024]{1,0:T(8,128)(2,1)S(1)}, bf16[512,1024]{1,0:T(8,128)(2,1)S(1)}, bf16[512,1024]{1,0:T(8,128)(2,1)S(1)}) custom-call(bf16[512,1024]{1,0:T(8,128)(2,1)S(1)} %copy-done.14, bf16[512,1024]{1,0:T(8,128)(2,1)S(1)} %copy-done.16, bf16[512,1024]{1,0:T(8,128)(2,1)} %copy-done.17, bf16[512,1024]{1,0:T(8,128)(2,1)} %fusion.21.g_ref, ...), custom_call_target="tpu_custom_call" | custom-call | flops 2684354560 | bytes 7340032 | tf_op jit(solution)/shard_map/pallas_call | solution.py:154
  338.0 2.4 collective-permute-done.20
  347.5 17.6 %collective-permute-start.43 = (bf16[256,1024]{1,0:T(8,128)(2,1)}, bf16[256,1024]{1,0:T(8,128)(2,1)}, u32[]{:S(2)}, u32[]{:S(2)}) collective-permute-start(bf16[256,1024]{1,0:T(8,128)(2,1)} %slice.307), channel_id=1, source_target_pairs={{0,8},{1,9},{2,10},{3,11},{4,12},{5,13},{6,14},{7,15},{8,0},{9,1},... | collective-permute-start | bytes 1572872 | tf_op jit(solution)/shard_map/ppermute | solution.py:304
  365.1 6.7 %fusion.2 = f32[512,1024]{1,0:T(8,128)} fusion(bf16[512,3072]{1,0:T(8,128)(2,1)} %constant_dynamic-update-slice_fusion.6.g_ref, bf16[1024,4096]{1,0:T(8,128)(2,1)S(1)} %bitcast.60), kind=kOutput, calls=%fused_computation.3 | convolution fusion | flops 3221225472 | bytes 11534336 | tf_op jit(solution)/shard_map/dot_general | solution.py:25
  375.6 2.8 shard_map.291
  382.3 2.5 add_convert_fusion.8
  387.0 2.5 fusion.62
  394.6 6.2 %shard_map.292 = bf16[512,3072]{1,0:T(8,128)(2,1)S(1)} custom-call(bf16[512,512]{1,0:T(8,128)(2,1)S(1)} %copy-done.7, bf16[512,512]{1,0:T(8,128)(2,1)} %collective-permute-done.31.xs_ref, bf16[512,3072]{1,0:T(8,128)(2,1)} %constant_dynamic-update-slice_fusion.6.g_ref, bf16[512,3072]{1,0:T(8,128)(2,1)} %collective-permute-done.34.gs_ref), custom_call_target="tpu_custom_call" | custom-call | flops 3221225472 | bytes 10485760 | tf_op jit(solution)/shard_map/pallas_call | solution.py:264
  403.5 5.0 shard_map.290
  411.8 10.1 %add_convert_fusion.5 = bf16[512,1024]{1,0:T(8,128)(2,1)} fusion(f32[512,1024]{1,0:T(8,128)S(1)} %copy-done.27, bf16[512,4096]{1,0:T(8,128)(2,1)} %get-tuple-element.55, bf16[4096,1024]{1,0:T(8,128)(2,1)} %all-gather.5.cloned.1.call-done.w_ref, f32[1024]{0:T(1024)S(1)} %copy-done.72), kind=kOutput, calls=%fused_computation.31 | convolution fusion | flops 4296540160 | bytes 15732736 | tf_op jit(solution)/shard_map/dot_general | solution.py:21
  423.4 5.2 %collective-permute-done.35 = bf16[256,4096]{1,0:T(8,128)(2,1)} collective-permute-done((bf16[256,4096]{1,0:T(8,128)(2,1)}, bf16[256,4096]{1,0:T(8,128)(2,1)}, u32[]{:S(2)}, u32[]{:S(2)}) %collective-permute-start.35) | collective-permute-done | bytes 2097184 | tf_op jit(solution)/shard_map/ppermute | solution.py:304
  431.7 17.7 %collective-permute-done.26 = bf16[576,1024]{1,0:T(8,128)(2,1)S(1)} collective-permute-done((bf16[576,1024]{1,0:T(8,128)(2,1)S(1)}, bf16[576,1024]{1,0:T(8,128)(2,1)S(1)}, u32[]{:S(2)}, u32[]{:S(2)}) %collective-permute-start.26) | collective-permute-done | bytes 1179680 | tf_op jit(solution)/shard_map/ppermute | solution.py:304
  453.9 2.7 collective-permute-start.41
  456.7 3.2 collective-permute-done.27
  460.1 4.6 collective-permute-start.28
  464.7 2.6 fusion.63
  467.3 4.2 collective-permute-done.28
  472.6 7.2 %collective-permute-start.37 = (bf16[64,4096]{1,0:T(8,128)(2,1)S(1)}, bf16[64,4096]{1,0:T(8,128)(2,1)S(1)}, u32[]{:S(2)}, u32[]{:S(2)}) collective-permute-start(bf16[64,4096]{1,0:T(8,128)(2,1)S(1)} %slice.294), channel_id=1, source_target_pairs={{0,8},{1,9},{2,10},{3,11},{4,12},{5,13},{6,14},{7,15},{24,16},{25,... | collective-permute-start | bytes 1572872 | tf_op jit(solution)/shard_map/ppermute | solution.py:304
  480.7 3.3 collective-permute-start.30
  484.0 7.4 %collective-permute-done.37 = bf16[64,4096]{1,0:T(8,128)(2,1)S(1)} collective-permute-done((bf16[64,4096]{1,0:T(8,128)(2,1)S(1)}, bf16[64,4096]{1,0:T(8,128)(2,1)S(1)}, u32[]{:S(2)}, u32[]{:S(2)}) %collective-permute-start.37) | collective-permute-done | bytes 524320 | tf_op jit(solution)/shard_map/ppermute | solution.py:304
  493.4 12.8 %collective-permute-start.39 = (bf16[32,4096]{1,0:T(8,128)(2,1)S(1)}, bf16[32,4096]{1,0:T(8,128)(2,1)S(1)}, u32[]{:S(2)}, u32[]{:S(2)}) collective-permute-start(bf16[32,4096]{1,0:T(8,128)(2,1)S(1)} %slice.296), channel_id=1, source_target_pairs={{0,8},{1,9},{2,10},{3,11},{4,12},{5,13},{6,14},{7,15},{8,0},{9,1},... | collective-permute-start | bytes 786440 | tf_op jit(solution)/shard_map/ppermute | solution.py:304
  508.0 2.5 collective-permute-done.39
  (360 shorter events, 113.3 us)
Async XLA Ops:
  7.2 206.0 %all-gather.3.cloned.1.call-start = ((), (), s32[]{:S(2)}) async-start(), calls=%async_computation | async-start | bytes 8650752 | tf_op jit(solution)/shard_map/all_gather | solution.py:466
  8.0 225.9 %all-gather.5.cloned.1.call-start = ((), (), s32[]{:S(2)}) async-start(), calls=%async_computation.1 | async-start | bytes 8650752 | tf_op jit(solution)/shard_map/all_gather | solution.py:467
  10.5 9.3 %collective-permute-start.7 = (bf16[32,4096]{1,0:T(8,128)(2,1)S(1)}, bf16[32,4096]{1,0:T(8,128)(2,1)S(1)}, u32[]{:S(2)}, u32[]{:S(2)}) collective-permute-start(bf16[32,4096]{1,0:T(8,128)(2,1)S(1)} %constant_dynamic-update-slice_fusion.4), channel_id=1, source_target_pairs={{0,8},{1,9},{2,10},{3,11},{4,12},{5,13},{6,14},{7,15},{8,0},{9,1},... | collective-permute-start | bytes 786440 | tf_op jit(solution)/shard_map/ppermute | solution.py:304
  19.9 0.7 collective-permute-start.8
  20.6 45.0 %collective-permute-start.9 = (bf16[64,4096]{1,0:T(8,128)(2,1)S(1)}, bf16[64,4096]{1,0:T(8,128)(2,1)S(1)}, u32[]{:S(2)}, u32[]{:S(2)}) collective-permute-start(bf16[64,4096]{1,0:T(8,128)(2,1)S(1)} %collective-permute-done.8), channel_id=1, source_target_pairs={{8,0},{9,1},{10,2},{11,3},{12,4},{13,5},{14,6},{15,7},{16,24},{17,... | collective-permute-start | bytes 1572872 | tf_op jit(solution)/shard_map/ppermute | solution.py:304
  22.1 59.0 %copy-start.51 = (bf16[8,1024]{1,0:T(8,128)(2,1)}, bf16[8,1024]{1,0:T(8,128)(2,1)S(1)}, u32[]{:S(2)}) copy-start(bf16[8,1024]{1,0:T(8,128)(2,1)S(1)} %reshape.458) | copy-start | bytes 49156
  22.1 6.3 %collective-permute-start = (bf16[72,1024]{1,0:T(8,128)(2,1)S(1)}, bf16[72,1024]{1,0:T(8,128)(2,1)S(1)}, u32[]{:S(2)}, u32[]{:S(2)}) collective-permute-start(bf16[72,1024]{1,0:T(8,128)(2,1)S(1)} %pad_maximum_fusion.10), channel_id=1, source_target_pairs={{0,2},{1,5},{2,0},{3,7},{4,6},{5,1},{6,4},{7,3},{8,10},{9,13},{10,... | collective-permute-start | bytes 442376 | tf_op jit(solution)/shard_map/ppermute | solution.py:304
  28.4 52.6 %collective-permute-start.1 = (bf16[144,1024]{1,0:T(8,128)(2,1)S(1)}, bf16[144,1024]{1,0:T(8,128)(2,1)S(1)}, u32[]{:S(2)}, u32[]{:S(2)}) collective-permute-start(bf16[144,1024]{1,0:T(8,128)(2,1)S(1)} %pad_maximum_fusion.9), channel_id=1, source_target_pairs={{0,8},{1,9},{2,10},{3,11},{4,12},{5,13},{6,14},{7,15},{8,0},{9,1},... | collective-permute-start | bytes 884744 | tf_op jit(solution)/shard_map/ppermute | solution.py:304
  65.8 28.5 %collective-permute-start.10 = (bf16[128,4096]{1,0:T(8,128)(2,1)S(1)}, bf16[128,4096]{1,0:T(8,128)(2,1)}, u32[]{:S(2)}, u32[]{:S(2)}) collective-permute-start(bf16[128,4096]{1,0:T(8,128)(2,1)S(1)} %pad_maximum_fusion.6), channel_id=1, source_target_pairs={{0,2},{1,5},{2,0},{3,7},{4,6},{5,1},{6,4},{7,3},{8,10},{9,13},{10,... | collective-permute-start | bytes 3145736 | tf_op jit(solution)/shard_map/ppermute | solution.py:304
  67.3 187.3 %collective-permute-start.16 = (bf16[512,1024]{1,0:T(8,128)(2,1)S(1)}, bf16[512,1024]{1,0:T(8,128)(2,1)}, u32[]{:S(2)}, u32[]{:S(2)}) collective-permute-start(bf16[512,1024]{1,0:T(8,128)(2,1)S(1)} %bitcast.52), channel_id=1, source_target_pairs={{0,1},{1,0},{2,3},{3,2},{4,5},{5,4},{6,7},{7,6},{8,9},{9,8},{10,11... | collective-permute-start | bytes 3145736 | tf_op jit(solution)/shard_map/ppermute | solution.py:304
  82.0 3.6 collective-permute-start.2
  85.6 38.0 %collective-permute-start.3 = (bf16[288,1024]{1,0:T(8,128)(2,1)}, bf16[288,1024]{1,0:T(8,128)(2,1)S(1)}, u32[]{:S(2)}, u32[]{:S(2)}) collective-permute-start(bf16[288,1024]{1,0:T(8,128)(2,1)} %collective-permute-done.2), channel_id=1, source_target_pairs={{8,0},{9,1},{10,2},{11,3},{12,4},{13,5},{14,6},{15,7},{16,24},{17,... | collective-permute-start | bytes 1769480 | tf_op jit(solution)/shard_map/ppermute | solution.py:304
  96.0 54.3 %collective-permute-start.11 = (bf16[256,4096]{1,0:T(8,128)(2,1)S(1)}, bf16[256,4096]{1,0:T(8,128)(2,1)}, u32[]{:S(2)}, u32[]{:S(2)}) collective-permute-start(bf16[256,4096]{1,0:T(8,128)(2,1)S(1)} %pad_maximum_fusion.3.refs_1_), channel_id=1, source_target_pairs={{0,4},{1,3},{2,6},{3,1},{4,0},{5,7},{6,2},{7,5},{8,12},{9,11},{10,... | collective-permute-start | bytes 6291464 | tf_op jit(solution)/shard_map/ppermute | solution.py:304
  127.3 20.3 %collective-permute-start.4 = (bf16[576,1024]{1,0:T(8,128)(2,1)}, bf16[576,1024]{1,0:T(8,128)(2,1)}, u32[]{:S(2)}, u32[]{:S(2)}) collective-permute-start(bf16[576,1024]{1,0:T(8,128)(2,1)} %constant_dynamic-update-slice_fusion.refs_1_), channel_id=1, source_target_pairs={{0,4},{1,3},{2,6},{3,1},{4,0},{5,7},{6,2},{7,5},{8,12},{9,11},{10,... | collective-permute-start | bytes 3538952 | tf_op jit(solution)/shard_map/ppermute | solution.py:304
  132.2 26.0 %collective-permute-start.6 = (bf16[576,1024]{1,0:T(8,128)(2,1)}, bf16[576,1024]{1,0:T(8,128)(2,1)S(1)}, u32[]{:S(2)}, u32[]{:S(2)}) collective-permute-start(bf16[576,1024]{1,0:T(8,128)(2,1)} %constant_dynamic-update-slice_fusion.refs_1_), channel_id=1, source_target_pairs={{0,1},{1,0},{2,3},{3,2},{4,5},{5,4},{6,7},{7,6},{8,9},{9,8},{10,11... | collective-permute-start | bytes 3538952 | tf_op jit(solution)/shard_map/ppermute | solution.py:304
  147.6 10.6 %collective-permute-start.5 = (bf16[576,1024]{1,0:T(8,128)(2,1)}, bf16[576,1024]{1,0:T(8,128)(2,1)S(1)}, u32[]{:S(2)}, u32[]{:S(2)}) collective-permute-start(bf16[576,1024]{1,0:T(8,128)(2,1)} %collective-permute-done.4.refs_0_), channel_id=1, source_target_pairs={{0,1},{1,0},{2,3},{3,2},{4,5},{5,4},{6,7},{7,6},{8,9},{9,8},{10,11... | collective-permute-start | bytes 3538952 | tf_op jit(solution)/shard_map/ppermute | solution.py:304
  149.7 30.7 %collective-permute-start.13 = (bf16[256,4096]{1,0:T(8,128)(2,1)S(1)}, bf16[256,4096]{1,0:T(8,128)(2,1)}, u32[]{:S(2)}, u32[]{:S(2)}) collective-permute-start(bf16[256,4096]{1,0:T(8,128)(2,1)S(1)} %pad_maximum_fusion.3.refs_1_), channel_id=1, source_target_pairs={{0,1},{1,0},{2,3},{3,2},{4,5},{5,4},{6,7},{7,6},{8,9},{9,8},{10,11... | collective-permute-start | bytes 6291464 | tf_op jit(solution)/shard_map/ppermute | solution.py:304
  150.3 30.1 %collective-permute-start.12 = (bf16[256,4096]{1,0:T(8,128)(2,1)}, bf16[256,4096]{1,0:T(8,128)(2,1)}, u32[]{:S(2)}, u32[]{:S(2)}) collective-permute-start(bf16[256,4096]{1,0:T(8,128)(2,1)} %collective-permute-done.11.refs_0_), channel_id=1, source_target_pairs={{0,1},{1,0},{2,3},{3,2},{4,5},{5,4},{6,7},{7,6},{8,9},{9,8},{10,11... | collective-permute-start | bytes 6291464 | tf_op jit(solution)/shard_map/ppermute | solution.py:304
  231.4 23.3 %collective-permute-start.15 = (bf16[512,2048]{1,0:T(8,128)(2,1)}, bf16[512,2048]{1,0:T(8,128)(2,1)}, u32[]{:S(2)}, u32[]{:S(2)}) collective-permute-start(bf16[512,2048]{1,0:T(8,128)(2,1)} %get-tuple-element.41), channel_id=1, source_target_pairs={{0,1},{1,0},{2,3},{3,2},{4,5},{5,4},{6,7},{7,6},{8,9},{9,8},{10,11... | collective-permute-start | bytes 6291464 | tf_op jit(solution)/shard_map/ppermute | solution.py:304
  245.0 60.0 %collective-permute-start.18 = (bf16[512,4096]{1,0:T(8,128)(2,1)}, bf16[512,4096]{1,0:T(8,128)(2,1)}, u32[]{:S(2)}, u32[]{:S(2)}) collective-permute-start(bf16[512,4096]{1,0:T(8,128)(2,1)} %get-tuple-element.43.g_ref), channel_id=1, source_target_pairs={{0,1},{1,0},{2,3},{3,2},{4,5},{5,4},{6,7},{7,6},{8,9},{9,8},{10,11... | collective-permute-start | bytes 12582920 | tf_op jit(solution)/shard_map/ppermute | solution.py:304
  254.3 50.8 %collective-permute-start.17 = (bf16[512,512]{1,0:T(8,128)(2,1)S(1)}, bf16[512,512]{1,0:T(8,128)(2,1)S(1)}, u32[]{:S(2)}, u32[]{:S(2)}) collective-permute-start(bf16[512,512]{1,0:T(8,128)(2,1)S(1)} %get-tuple-element.124), channel_id=1, source_target_pairs={{0,1},{1,0},{2,3},{3,2},{4,5},{5,4},{6,7},{7,6},{8,9},{9,8},{10,11... | collective-permute-start | bytes 1572872 | tf_op jit(solution)/shard_map/ppermute | solution.py:304
  265.3 26.1 %collective-permute-start.19 = (bf16[1024,1024]{1,0:T(8,128)(2,1)S(1)}, bf16[1024,1024]{1,0:T(8,128)(2,1)S(1)}, u32[]{:S(2)}, u32[]{:S(2)}) collective-permute-start(bf16[1024,1024]{1,0:T(8,128)(2,1)S(1)} %slice.262), channel_id=1, source_target_pairs={{0,4},{1,3},{2,6},{3,1},{4,0},{5,7},{6,2},{7,5},{8,12},{9,11},{10,... | collective-permute-start | bytes 6291464 | tf_op jit(solution)/shard_map/ppermute | solution.py:304
  269.4 102.4 %collective-permute-start.32 = (bf16[512,512]{1,0:T(8,128)(2,1)}, bf16[512,512]{1,0:T(8,128)(2,1)}, u32[]{:S(2)}, u32[]{:S(2)}) collective-permute-start(bf16[512,512]{1,0:T(8,128)(2,1)} %get-tuple-element.122), channel_id=1, source_target_pairs={{0,1},{1,0},{2,3},{3,2},{4,5},{5,4},{6,7},{7,6},{8,9},{9,8},{10,11... | collective-permute-start | bytes 1572872 | tf_op jit(solution)/shard_map/ppermute | solution.py:304
  293.6 43.1 %collective-permute-start.22 = (bf16[512,1024]{1,0:T(8,128)(2,1)}, bf16[512,1024]{1,0:T(8,128)(2,1)S(1)}, u32[]{:S(2)}, u32[]{:S(2)}) collective-permute-start(bf16[512,1024]{1,0:T(8,128)(2,1)} %slice.267), channel_id=1, source_target_pairs={{0,8},{1,9},{2,10},{3,11},{4,12},{5,13},{6,14},{7,15},{24,16},{25,... | collective-permute-start | bytes 3145736 | tf_op jit(solution)/shard_map/ppermute | solution.py:304
  314.0 26.4 %collective-permute-start.20 = (bf16[256,4096]{1,0:T(8,128)(2,1)}, bf16[256,4096]{1,0:T(8,128)(2,1)}, u32[]{:S(2)}, u32[]{:S(2)}) collective-permute-start(bf16[256,4096]{1,0:T(8,128)(2,1)} %slice.264), channel_id=1, source_target_pairs={{0,4},{1,3},{2,6},{3,1},{4,0},{5,7},{6,2},{7,5},{8,12},{9,11},{10,... | collective-permute-start | bytes 6291464 | tf_op jit(solution)/shard_map/ppermute | solution.py:304
  317.3 54.6 %collective-permute-start.33 = (bf16[512,1024]{1,0:T(8,128)(2,1)S(1)}, bf16[512,1024]{1,0:T(8,128)(2,1)S(1)}, u32[]{:S(2)}, u32[]{:S(2)}) collective-permute-start(bf16[512,1024]{1,0:T(8,128)(2,1)S(1)} %fusion.61.g_ref), channel_id=1, source_target_pairs={{0,1},{1,0},{2,3},{3,2},{4,5},{5,4},{6,7},{7,6},{8,9},{9,8},{10,11... | collective-permute-start | bytes 3145736 | tf_op jit(solution)/shard_map/ppermute | solution.py:304
  336.3 58.3 %collective-permute-start.34 = (bf16[512,3072]{1,0:T(8,128)(2,1)}, bf16[512,3072]{1,0:T(8,128)(2,1)}, u32[]{:S(2)}, u32[]{:S(2)}) collective-permute-start(bf16[512,3072]{1,0:T(8,128)(2,1)} %constant_dynamic-update-slice_fusion.6.g_ref), channel_id=1, source_target_pairs={{0,1},{1,0},{2,3},{3,2},{4,5},{5,4},{6,7},{7,6},{8,9},{9,8},{10,11... | collective-permute-start | bytes 9437192 | tf_op jit(solution)/shard_map/ppermute | solution.py:304
  337.1 9.1 %collective-permute-start.23 = (bf16[512,1024]{1,0:T(8,128)(2,1)S(1)}, bf16[512,1024]{1,0:T(8,128)(2,1)S(1)}, u32[]{:S(2)}, u32[]{:S(2)}) collective-permute-start(bf16[512,1024]{1,0:T(8,128)(2,1)S(1)} %add_convert_fusion.7), channel_id=1, source_target_pairs={{8,16},{9,17},{10,18},{11,19},{12,20},{13,21},{14,22},{15,23},{16,... | collective-permute-start | bytes 3145736 | tf_op jit(solution)/shard_map/ppermute | solution.py:304
  344.0 38.3 %collective-permute-start.21 = (bf16[128,4096]{1,0:T(8,128)(2,1)}, bf16[128,4096]{1,0:T(8,128)(2,1)}, u32[]{:S(2)}, u32[]{:S(2)}) collective-permute-start(bf16[128,4096]{1,0:T(8,128)(2,1)} %slice.265), channel_id=1, source_target_pairs={{0,8},{1,9},{2,10},{3,11},{4,12},{5,13},{6,14},{7,15},{24,16},{25,... | collective-permute-start | bytes 3145736 | tf_op jit(solution)/shard_map/ppermute | solution.py:304
  347.5 31.5 %collective-permute-start.43 = (bf16[256,1024]{1,0:T(8,128)(2,1)}, bf16[256,1024]{1,0:T(8,128)(2,1)}, u32[]{:S(2)}, u32[]{:S(2)}) collective-permute-start(bf16[256,1024]{1,0:T(8,128)(2,1)} %slice.307), channel_id=1, source_target_pairs={{0,8},{1,9},{2,10},{3,11},{4,12},{5,13},{6,14},{7,15},{8,0},{9,1},... | collective-permute-start | bytes 1572872 | tf_op jit(solution)/shard_map/ppermute | solution.py:304
  371.9 31.6 %collective-permute-start.14 = (bf16[512,1024]{1,0:T(8,128)(2,1)}, bf16[512,1024]{1,0:T(8,128)(2,1)}, u32[]{:S(2)}, u32[]{:S(2)}) collective-permute-start(bf16[512,1024]{1,0:T(8,128)(2,1)} %get-tuple-element.118), channel_id=1, source_target_pairs={{0,1},{1,0},{2,3},{3,2},{4,5},{5,4},{6,7},{7,6},{8,9},{9,8},{10,11... | collective-permute-start | bytes 3145736 | tf_op jit(solution)/shard_map/ppermute | solution.py:304
  372.9 21.1 %collective-permute-start.31 = (bf16[512,512]{1,0:T(8,128)(2,1)}, bf16[512,512]{1,0:T(8,128)(2,1)}, u32[]{:S(2)}, u32[]{:S(2)}) collective-permute-start(bf16[512,512]{1,0:T(8,128)(2,1)} %get-tuple-element.120), channel_id=1, source_target_pairs={{0,1},{1,0},{2,3},{3,2},{4,5},{5,4},{6,7},{7,6},{8,9},{9,8},{10,11... | collective-permute-start | bytes 1572872 | tf_op jit(solution)/shard_map/ppermute | solution.py:304
  380.5 9.1 %collective-permute-start.44 = (bf16[128,1024]{1,0:T(8,128)(2,1)S(1)}, bf16[128,1024]{1,0:T(8,128)(2,1)S(1)}, u32[]{:S(2)}, u32[]{:S(2)}) collective-permute-start(bf16[128,1024]{1,0:T(8,128)(2,1)S(1)} %slice.309), channel_id=1, source_target_pairs={{0,2},{1,5},{2,0},{3,7},{4,6},{5,1},{6,4},{7,3},{8,10},{9,13},{10,... | collective-permute-start | bytes 786440 | tf_op jit(solution)/shard_map/ppermute | solution.py:304
  389.5 13.9 %collective-permute-start.24 = (bf16[512,1024]{1,0:T(8,128)(2,1)S(1)}, bf16[512,1024]{1,0:T(8,128)(2,1)}, u32[]{:S(2)}, u32[]{:S(2)}) collective-permute-start(bf16[512,1024]{1,0:T(8,128)(2,1)S(1)} %get-tuple-element.56.g_ref), channel_id=1, source_target_pairs={{0,1},{1,0},{2,3},{3,2},{4,5},{5,4},{6,7},{7,6},{8,9},{9,8},{10,11... | collective-permute-start | bytes 3145736 | tf_op jit(solution)/shard_map/ppermute | solution.py:304
  390.4 31.5 %collective-permute-start.40 = (bf16[128,4096]{1,0:T(8,128)(2,1)}, bf16[128,4096]{1,0:T(8,128)(2,1)}, u32[]{:S(2)}, u32[]{:S(2)}) collective-permute-start(bf16[128,4096]{1,0:T(8,128)(2,1)} %add_convert_fusion.8), channel_id=1, source_target_pairs={{8,16},{9,17},{10,18},{11,19},{12,20},{13,21},{14,22},{15,23},{16,... | collective-permute-start | bytes 3145736 | tf_op jit(solution)/shard_map/ppermute | solution.py:304
  394.0 9.1 %collective-permute-start.25 = (f32[32,256]{1,0:T(8,128)S(1)}, f32[32,256]{1,0:T(8,128)S(1)}, u32[]{:S(2)}, u32[]{:S(2)}) collective-permute-start(f32[32,256]{1,0:T(8,128)S(1)} %concatenate.74), channel_id=1, source_target_pairs={{0,1},{1,0},{2,3},{3,2},{4,5},{5,4},{6,7},{7,6},{8,9},{9,8},{10,11... | collective-permute-start | bytes 98312 | tf_op jit(solution)/shard_map/ppermute | solution.py:304
  402.3 26.4 %collective-permute-start.35 = (bf16[256,4096]{1,0:T(8,128)(2,1)}, bf16[256,4096]{1,0:T(8,128)(2,1)}, u32[]{:S(2)}, u32[]{:S(2)}) collective-permute-start(bf16[256,4096]{1,0:T(8,128)(2,1)} %pad_maximum_fusion.1), channel_id=1, source_target_pairs={{0,4},{1,3},{2,6},{3,1},{4,0},{5,7},{6,2},{7,5},{8,12},{9,11},{10,... | collective-permute-start | bytes 6291464 | tf_op jit(solution)/shard_map/ppermute | solution.py:304
  410.5 38.8 %collective-permute-start.26 = (bf16[576,1024]{1,0:T(8,128)(2,1)S(1)}, bf16[576,1024]{1,0:T(8,128)(2,1)S(1)}, u32[]{:S(2)}, u32[]{:S(2)}) collective-permute-start(bf16[576,1024]{1,0:T(8,128)(2,1)S(1)} %bitcast.67), channel_id=1, source_target_pairs={{0,4},{1,3},{2,6},{3,1},{4,0},{5,7},{6,2},{7,5},{8,12},{9,11},{10,... | collective-permute-start | bytes 3538952 | tf_op jit(solution)/shard_map/ppermute | solution.py:304
  431.1 41.2 %collective-permute-start.36 = (bf16[128,4096]{1,0:T(8,128)(2,1)S(1)}, bf16[128,4096]{1,0:T(8,128)(2,1)S(1)}, u32[]{:S(2)}, u32[]{:S(2)}) collective-permute-start(bf16[128,4096]{1,0:T(8,128)(2,1)S(1)} %slice.292), channel_id=1, source_target_pairs={{0,2},{1,5},{2,0},{3,7},{4,6},{5,1},{6,4},{7,3},{8,10},{9,13},{10,... | collective-permute-start | bytes 3145736 | tf_op jit(solution)/shard_map/ppermute | solution.py:304
  449.9 9.9 %collective-permute-start.27 = (bf16[288,1024]{1,0:T(8,128)(2,1)S(1)}, bf16[288,1024]{1,0:T(8,128)(2,1)S(1)}, u32[]{:S(2)}, u32[]{:S(2)}) collective-permute-start(bf16[288,1024]{1,0:T(8,128)(2,1)S(1)} %slice.276), channel_id=1, source_target_pairs={{0,2},{1,5},{2,0},{3,7},{4,6},{5,1},{6,4},{7,3},{8,10},{9,13},{10,... | collective-permute-start | bytes 1769480 | tf_op jit(solution)/shard_map/ppermute | solution.py:304
  453.9 25.9 %collective-permute-start.41 = (bf16[64,4096]{1,0:T(8,128)(2,1)S(1)}, bf16[64,4096]{1,0:T(8,128)(2,1)S(1)}, u32[]{:S(2)}, u32[]{:S(2)}) collective-permute-start(bf16[64,4096]{1,0:T(8,128)(2,1)S(1)} %slice.302), channel_id=1, source_target_pairs={{0,8},{1,9},{2,10},{3,11},{4,12},{5,13},{6,14},{7,15},{8,0},{9,1},... | collective-permute-start | bytes 1572872 | tf_op jit(solution)/shard_map/ppermute | solution.py:304
  460.1 11.4 %collective-permute-start.28 = (bf16[144,1024]{1,0:T(8,128)(2,1)S(1)}, bf16[144,1024]{1,0:T(8,128)(2,1)S(1)}, u32[]{:S(2)}, u32[]{:S(2)}) collective-permute-start(bf16[144,1024]{1,0:T(8,128)(2,1)S(1)} %slice.278), channel_id=1, source_target_pairs={{0,8},{1,9},{2,10},{3,11},{4,12},{5,13},{6,14},{7,15},{24,16},{25,... | collective-permute-start | bytes 884744 | tf_op jit(solution)/shard_map/ppermute | solution.py:304
  471.6 9.0 %collective-permute-start.29 = (bf16[144,1024]{1,0:T(8,128)(2,1)S(1)}, bf16[144,1024]{1,0:T(8,128)(2,1)S(1)}, u32[]{:S(2)}, u32[]{:S(2)}) collective-permute-start(bf16[144,1024]{1,0:T(8,128)(2,1)S(1)} %add_convert_fusion.15), channel_id=1, source_target_pairs={{8,16},{9,17},{10,18},{11,19},{12,20},{13,21},{14,22},{15,23},{16,... | collective-permute-start | bytes 884744 | tf_op jit(solution)/shard_map/ppermute | solution.py:304
  472.6 18.8 %collective-permute-start.37 = (bf16[64,4096]{1,0:T(8,128)(2,1)S(1)}, bf16[64,4096]{1,0:T(8,128)(2,1)S(1)}, u32[]{:S(2)}, u32[]{:S(2)}) collective-permute-start(bf16[64,4096]{1,0:T(8,128)(2,1)S(1)} %slice.294), channel_id=1, source_target_pairs={{0,8},{1,9},{2,10},{3,11},{4,12},{5,13},{6,14},{7,15},{24,16},{25,... | collective-permute-start | bytes 1572872 | tf_op jit(solution)/shard_map/ppermute | solution.py:304
  480.0 12.2 %collective-permute-start.42 = (bf16[32,4096]{1,0:T(8,128)(2,1)S(1)}, bf16[32,4096]{1,0:T(8,128)(2,1)S(1)}, u32[]{:S(2)}, u32[]{:S(2)}) collective-permute-start(bf16[32,4096]{1,0:T(8,128)(2,1)S(1)} %slice.304), channel_id=1, source_target_pairs={{0,2},{1,5},{2,0},{3,7},{4,6},{5,1},{6,4},{7,3},{8,10},{9,13},{10,... | collective-permute-start | bytes 786440 | tf_op jit(solution)/shard_map/ppermute | solution.py:304
  480.7 12.4 %collective-permute-start.30 = (bf16[72,1024]{1,0:T(8,128)(2,1)S(1)}, bf16[72,1024]{1,0:T(8,128)(2,1)S(1)}, u32[]{:S(2)}, u32[]{:S(2)}) collective-permute-start(bf16[72,1024]{1,0:T(8,128)(2,1)S(1)} %slice.280), channel_id=1, source_target_pairs={{0,8},{1,9},{2,10},{3,11},{4,12},{5,13},{6,14},{7,15},{8,0},{9,1},... | collective-permute-start | bytes 442376 | tf_op jit(solution)/shard_map/ppermute | solution.py:304
  491.6 1.6 collective-permute-start.38
  493.4 17.2 %collective-permute-start.39 = (bf16[32,4096]{1,0:T(8,128)(2,1)S(1)}, bf16[32,4096]{1,0:T(8,128)(2,1)S(1)}, u32[]{:S(2)}, u32[]{:S(2)}) collective-permute-start(bf16[32,4096]{1,0:T(8,128)(2,1)S(1)} %slice.296), channel_id=1, source_target_pairs={{0,8},{1,9},{2,10},{3,11},{4,12},{5,13},{6,14},{7,15},{8,0},{9,1},... | collective-permute-start | bytes 786440 | tf_op jit(solution)/shard_map/ppermute | solution.py:304
  (83 other events, 948.7 us)
Sparse Core Ops, SparseCore 0:
  10.9 96.8 all-gather.2
  110.7 79.9 all-gather.4
